TPU v7x, 256 devices: a whole 4x4x8 slice. The times are simulated.
256 devices in a mesh: section: 4 (over z_hi), mp: 8 (over z_lo, y), seq: 8 (over x, core).
Axes of the slice: x: 4, y: 4, z: 8 (z_hi: 4, z_lo: 2; z = z_hi * 2 + z_lo), core: 2. Of those that a mesh axis runs over, the one named last changes fastest.
Arguments:
- prompt_queries: bfloat16 [4, 2, 1024, 8192], P('section', None, 'seq', 'mp'), may hold values from -8 to 8
- prompt_pairs: bfloat16 [4, 2, 1024, 2, 1024], P('section', None, 'seq', None, 'mp'), may hold values from -10 to 10
- decode_queries: bfloat16 [4, 128, 4, 8192], P('section', None, None, 'mp'), may hold values from -8 to 8
- decode_pairs: bfloat16 [4, 128, 4, 2, 1024], P('section', None, None, None, 'mp'), may hold values from -10 to 10
- cache_pool: bfloat16 [4, 384, 128, 2, 1024], P('section', 'seq', None, None, 'mp'), may hold values from -10 to 10
- out_weight: bfloat16 [4, 8192, 8192], P('section', 'mp', 'seq'), may hold values from -0.0625 to 0.0625
- slot_pages: int32 [384], P('seq'), may hold values from -1 to 131071, as said below
- placement: int32 [16], replicated, may hold values from 0 to 383, as said below
- context_len: int32 [128], replicated, may hold values from 2 to 2048, as said below
Outputs:
- prefill_out: bfloat16 [4, 2, 1024, 8192], P('section', None, 'seq', 'mp')
- decode_mix: bfloat16 [4, 128, 4, 8192], P('section', 'mp', None, 'seq')
Inputs may be any that keep to these rules, and one draw needn't show every extreme that they name: placement[p] = owner * 48 + slot; all entries differ and name slots that slot_pages marks free. The 2 pages whose positions lie in one index of seq's part of the prompt blocks both go to one owner; several indices of seq may send to the same owner. `slot_pages`: -1 marks a free slot; any other entry is r * 1024 + k with 1 <= r < 128: the slot holds page k of decode row r. Every row r >= 1 has its pages 0 to n_r - 1 each in one slot, n_r >= 1. Row 0 is the prefilled request: context_len[0] = 2048 and its pages are those of placement. For r >= 1, (n_r - 1) * 128 + 2 <= context_len[r] <= n_r * 128.
All inputs are finite; a program needn't handle non-finite values.
Results may differ from a plain program's by a relative error of at most 0.024.
Values may be sent and summed in bfloat16 or wider, within the bound.
A program may use at most 128 MiB of HBM per device.

v0:
```python
import math

import jax
import jax.numpy as jnp
from jax import lax
from jax.sharding import PartitionSpec as P

HEAD_SIZE = 128
MAXP = 1024
PROMPT_BLOCKS = 2


MASKED_SCORE = -1e30


def passed_along(x, axis, by):
    peers = lax.axis_size(axis)
    return lax.ppermute(x, axis, [(i, (i + by) % peers) for i in range(peers)])


def absorb_block(state_in, scores, allowed, value_matrix):
    running_max, running_sum, running_acc = state_in
    scores = jnp.where(allowed, scores, MASKED_SCORE)
    fresh_max = jnp.maximum(running_max, jnp.max(scores, axis=-1))
    attention_weight = jnp.where(allowed, jnp.exp(scores - fresh_max[..., None]), 0.0)
    keep_factor = jnp.exp(running_max - fresh_max)
    running_sum = running_sum * keep_factor + jnp.sum(attention_weight, axis=-1)
    update = jnp.einsum(
        "igqj,jgd->igqd",
        attention_weight.astype(jnp.bfloat16),
        value_matrix,
        preferred_element_type=jnp.float32,
    )
    running_acc = running_acc * keep_factor[..., None] + update
    return (fresh_max, running_sum, running_acc)


def prefill_segment(query_shard, pair_shard):
    query_matrix = query_shard[0]
    key_value_pairs = pair_shard[0]
    seq_index = lax.axis_index("seq")
    length = query_matrix.shape[1]
    q_width = query_matrix.shape[2]
    half_rows = length // 2
    pair_width = key_value_pairs.shape[3]
    kv_heads = pair_width // HEAD_SIZE
    query_group_width = q_width // pair_width
    score_scale = 1.0 / math.sqrt(HEAD_SIZE)
    offsets = jnp.arange(length, dtype=jnp.int32)
    query_pos = seq_index * length + offsets
    reshaped_input = query_matrix.reshape(
        PROMPT_BLOCKS, 2, half_rows, kv_heads, query_group_width, HEAD_SIZE
    )
    halves_pos = query_pos.reshape(2, half_rows)
    halves_last = jnp.max(halves_pos, axis=1)

    def fold_piece(states, key_piece, start_row):
        piece_rows = key_piece.shape[1]
        key_matrix = key_piece[:, :, 0].reshape(PROMPT_BLOCKS, piece_rows, kv_heads, HEAD_SIZE)
        value_matrix = key_piece[:, :, 1].reshape(PROMPT_BLOCKS, piece_rows, kv_heads, HEAD_SIZE)
        key_pos = jnp.arange(piece_rows, dtype=jnp.int32)
        updated = []
        for block_index in range(PROMPT_BLOCKS):
            halves = []
            for half_index in range(2):
                half_state = states[block_index][half_index]
                if block_index > 0:
                    past_keys = key_matrix[:block_index].reshape(
                        block_index * piece_rows, kv_heads, HEAD_SIZE
                    )
                    past_values = value_matrix[:block_index].reshape(
                        block_index * piece_rows, kv_heads, HEAD_SIZE
                    )
                    scores = (
                        jnp.einsum(
                            "igqd,jgd->igqj",
                            reshaped_input[block_index, half_index],
                            past_keys,
                            preferred_element_type=jnp.float32,
                        )
                        * score_scale
                    )
                    half_state = absorb_block(half_state, scores, True, past_values)

                def same_block(current, block_index=block_index, half_index=half_index):
                    allowed = (key_pos[None, :] <= halves_pos[half_index][:, None])[
                        :, None, None, :
                    ]
                    scores = (
                        jnp.einsum(
                            "igqd,jgd->igqj",
                            reshaped_input[block_index, half_index],
                            key_matrix[block_index],
                            preferred_element_type=jnp.float32,
                        )
                        * score_scale
                    )
                    return absorb_block(current, scores, allowed, value_matrix[block_index])

                def unchanged(current):
                    return current

                half_state = lax.cond(
                    start_row <= halves_last[half_index], same_block, unchanged, half_state
                )
                halves.append(half_state)
            updated.append(tuple(halves))
        return tuple(updated)

    empty_max = jnp.full((half_rows, kv_heads, query_group_width), MASKED_SCORE, jnp.float32)
    empty_sum = jnp.zeros((half_rows, kv_heads, query_group_width), jnp.float32)
    empty_acc = jnp.zeros((half_rows, kv_heads, query_group_width, HEAD_SIZE), jnp.float32)
    initial = tuple(
        (
            tuple(((empty_max, empty_sum, empty_acc) for half_index in range(2)))
            for block_index in range(PROMPT_BLOCKS)
        )
    )
    finals = fold_piece(
        initial, lax.all_gather(key_value_pairs, "seq", axis=1, tiled=True), jnp.int32(0)
    )
    results = []
    for block_index in range(PROMPT_BLOCKS):
        for half_index in range(2):
            final_max, final_sum, final_acc = finals[block_index][half_index]
            results.append((final_acc / final_sum[..., None]).astype(jnp.bfloat16))
    attended = jnp.stack(results).reshape(PROMPT_BLOCKS, length, q_width)
    return attended[None]


def deliver_pages(pair_shard, placement, slot_pages, pool_shard):
    key_value_pairs = pair_shard[0]
    pool_pages = pool_shard[0]
    seq_count = lax.axis_size("seq")
    seq_index = lax.axis_index("seq")
    length = key_value_pairs.shape[1]
    slot_count = pool_pages.shape[0]
    page_rows = pool_pages.shape[1]
    block_pages = length // page_rows
    device_pages = PROMPT_BLOCKS * block_pages
    capacity = max(2, device_pages // seq_count)
    targets = jnp.transpose(
        placement.reshape(PROMPT_BLOCKS, seq_count, block_pages), (1, 0, 2)
    ).reshape(seq_count, device_pages)
    owners = targets // slot_count
    page_ids = jnp.arange(device_pages, dtype=jnp.int32)
    earlier = page_ids[None, :] < page_ids[:, None]
    ranks = jnp.sum((owners[:, :, None] == owners[:, None, :]) & earlier[None], axis=2)
    my_owners = lax.dynamic_index_in_dim(owners, seq_index, 0, keepdims=False)
    my_ranks = lax.dynamic_index_in_dim(ranks, seq_index, 0, keepdims=False)
    dest_ids = jnp.arange(seq_count, dtype=jnp.int32)
    slot_ranks = jnp.arange(capacity, dtype=jnp.int32)
    matches = (my_owners[None, None, :] == dest_ids[:, None, None]) & (
        my_ranks[None, None, :] == slot_ranks[None, :, None]
    )
    occupied = jnp.any(matches, axis=2)
    source_page = jnp.sum(jnp.where(matches, page_ids[None, None, :], 0), axis=2)
    outgoing = jnp.where(
        occupied[:, :, None, None, None], key_value_pairs[source_page], jnp.zeros((), jnp.bfloat16)
    )
    half_turn = lax.axis_size("section") // 2
    arrived = lax.all_to_all(outgoing, "seq", split_axis=0, concat_axis=0, tiled=True)
    arrived = passed_along(arrived, "section", half_turn)
    fresh_ids = jnp.transpose(
        jnp.arange(PROMPT_BLOCKS * seq_count * block_pages, dtype=jnp.int32).reshape(
            PROMPT_BLOCKS, seq_count, block_pages
        ),
        (1, 0, 2),
    ).reshape(seq_count, device_pages)
    slot_ids = jnp.arange(slot_count, dtype=jnp.int32)
    hits = (owners == seq_index)[None] & ((targets % slot_count)[None] == slot_ids[:, None, None])
    filled = jnp.any(hits, axis=(1, 2))
    from_source = jnp.sum(jnp.where(hits, dest_ids[None, :, None], 0), axis=(1, 2))
    from_rank = jnp.sum(jnp.where(hits, ranks[None], 0), axis=(1, 2))
    from_fresh = jnp.sum(jnp.where(hits, fresh_ids[None], 0), axis=(1, 2))
    incoming = arrived[from_source, from_rank]
    pool_now = jnp.where(filled[:, None, None, None], incoming, pool_pages)
    entries = jnp.where(filled, from_fresh, slot_pages)
    return (pool_now, entries)


def finish_rows(
    top_max, total_sum, total_acc, reshaped_input, incoming_keys, incoming_values, score_scale
):
    step_count = reshaped_input.shape[1]
    recent = (
        jnp.einsum(
            "rtgqd,rugd->rtgqu", reshaped_input, incoming_keys, preferred_element_type=jnp.float32
        )
        * score_scale
    )
    step_ids = jnp.arange(step_count, dtype=jnp.int32)
    causal = (step_ids[None, :] <= step_ids[:, None])[None, :, None, None, :]
    recent = jnp.where(causal, recent, MASKED_SCORE)
    final_max = jnp.maximum(top_max, jnp.max(recent, axis=-1))
    carry_factor = jnp.exp(top_max - final_max)
    recent_weights = jnp.where(causal, jnp.exp(recent - final_max[..., None]), 0.0)
    total_sum = total_sum * carry_factor + jnp.sum(recent_weights, axis=-1)
    total_acc = total_acc * carry_factor[..., None] + jnp.einsum(
        "rtgqu,rugd->rtgqd",
        recent_weights.astype(jnp.bfloat16),
        incoming_values,
        preferred_element_type=jnp.float32,
    )
    return (total_acc / total_sum[..., None]).astype(jnp.bfloat16)


def decode_group(query_shard, new_shard, pool_now, entries, context_len, weight_shard):
    query_matrix = query_shard[0]
    incoming_pairs = new_shard[0]
    row_count = query_matrix.shape[0]
    step_count = query_matrix.shape[1]
    q_width = query_matrix.shape[2]
    slot_count = pool_now.shape[0]
    page_rows = pool_now.shape[1]
    pair_width = pool_now.shape[3]
    kv_heads = pair_width // HEAD_SIZE
    query_group_width = q_width // pair_width
    score_scale = 1.0 / math.sqrt(HEAD_SIZE)
    live_slot = entries >= 0
    owning_row = jnp.where(live_slot, entries // MAXP, 0)
    page_number = jnp.where(live_slot, entries % MAXP, 0)
    valid_rows = jnp.where(
        live_slot, jnp.clip(context_len[owning_row] - page_number * page_rows, 0, page_rows), 0
    )
    slotted_queries = query_matrix[owning_row].reshape(
        slot_count, step_count, kv_heads, query_group_width, HEAD_SIZE
    )
    slotted_keys = pool_now[:, :, 0].reshape(slot_count, page_rows, kv_heads, HEAD_SIZE)
    slotted_values = pool_now[:, :, 1].reshape(slot_count, page_rows, kv_heads, HEAD_SIZE)
    scores = (
        jnp.einsum(
            "stgqd,sjgd->stgqj", slotted_queries, slotted_keys, preferred_element_type=jnp.float32
        )
        * score_scale
    )
    allowed = (jnp.arange(page_rows, dtype=jnp.int32)[None, :] < valid_rows[:, None])[
        :, None, None, None, :
    ]
    scores = jnp.where(allowed, scores, MASKED_SCORE)
    slot_max = jnp.max(scores, axis=-1)
    attention_weight = jnp.where(allowed, jnp.exp(scores - slot_max[..., None]), 0.0)
    slot_sum = jnp.sum(attention_weight, axis=-1)
    slot_acc = jnp.einsum(
        "stgqj,sjgd->stgqd",
        attention_weight.astype(jnp.bfloat16),
        slotted_values,
        preferred_element_type=jnp.float32,
    )
    member = (owning_row[None, :] == jnp.arange(row_count, dtype=jnp.int32)[:, None]) & live_slot[
        None, :
    ]
    local_max = jnp.max(
        jnp.where(member[:, :, None, None, None], slot_max[None], MASKED_SCORE), axis=1
    )
    factor = jnp.exp(slot_max - local_max[owning_row])
    indicator_matrix = member.astype(jnp.float32)
    local_sum = jnp.dot(
        indicator_matrix,
        (slot_sum * factor).reshape(slot_count, -1),
        precision=lax.Precision.HIGHEST,
    ).reshape(local_max.shape)
    local_acc = jnp.dot(
        indicator_matrix,
        (slot_acc * factor[..., None]).reshape(slot_count, -1),
        precision=lax.Precision.HIGHEST,
    ).reshape(local_max.shape + (HEAD_SIZE,))
    reshaped_input = query_matrix.reshape(
        row_count, step_count, kv_heads, query_group_width, HEAD_SIZE
    )
    incoming_keys = incoming_pairs[:, :, 0].reshape(row_count, step_count, kv_heads, HEAD_SIZE)
    incoming_values = incoming_pairs[:, :, 1].reshape(row_count, step_count, kv_heads, HEAD_SIZE)
    top_max = lax.pmax(local_max, "seq")
    shrink = jnp.exp(local_max - top_max)
    total_sum, total_acc = (
        lax.psum((local_sum * shrink).astype(jnp.bfloat16), "seq").astype(jnp.float32),
        lax.psum((local_acc * shrink[..., None]).astype(jnp.bfloat16), "seq").astype(jnp.float32),
    )
    attended = finish_rows(
        top_max, total_sum, total_acc, reshaped_input, incoming_keys, incoming_values, score_scale
    )
    attended = attended.reshape(row_count, step_count, q_width)
    share_rows = row_count // lax.axis_size("mp")
    weight_matrix = weight_shard[0]
    picked = attended.reshape(lax.axis_size("mp") * share_rows * step_count, q_width)
    product = jnp.dot(picked, weight_matrix, preferred_element_type=jnp.float32)
    mixed = lax.psum_scatter(
        product.reshape(
            lax.axis_size("mp") * share_rows, step_count, weight_matrix.shape[1]
        ).astype(jnp.bfloat16),
        "mp",
        scatter_dimension=0,
        tiled=True,
    )
    return mixed[None]


def body(
    prompt_queries,
    prompt_pairs,
    decode_queries,
    decode_pairs,
    cache_pool,
    out_weight,
    slot_pages,
    placement,
    context_len,
):
    pool_now, entries = deliver_pages(prompt_pairs, placement, slot_pages, cache_pool)
    prefill_out = prefill_segment(prompt_queries, prompt_pairs)
    decode_mix = decode_group(
        decode_queries, decode_pairs, pool_now, entries, context_len, out_weight
    )
    return (prefill_out, decode_mix)


def solution(mesh):
    return jax.shard_map(
        body,
        mesh=mesh,
        in_specs=(
            P("section", None, "seq", "mp"),
            P("section", None, "seq", None, "mp"),
            P("section", None, None, "mp"),
            P("section", None, None, None, "mp"),
            P("section", "seq", None, None, "mp"),
            P("section", "mp", "seq"),
            P("seq"),
            P(),
            P(),
        ),
        out_specs=(P("section", None, "seq", "mp"), P("section", "mp", None, "seq")),
        check_vma=False,
    )
```

profile of v0, /device:TPU:1, one launch (start us, length us, event | category | flops | bytes accessed | tf_op | source)
XLA Modules:
  0.0 279.2 jit_solution(14381699452964760172)
XLA Ops:
  9.8 4.5 %gather_fusion = bf16[16,128,2,128]{3,2,1,0:T(2,128)(2,1)} fusion(bf16[2,128,2,128]{3,2,1,0:T(2,128)(2,1)} %bitcast.549, s32[1024]{0:T(1024)S(1)} %pad_clamp_fusion.1), kind=kCustom, calls=%fused_computation | custom fusion | bytes 2097216 | tf_op jit(solution)/shard_map/gather | solution.py:159
  14.3 2.5 copy.175
  16.9 2.4 broadcast_select_fusion
  19.3 7.5 %all-to-all-start = ((bf16[8,2,128,2,128]{4,2,3,1,0:T(8,128)(2,1)}), bf16[8,2,128,2,128]{4,2,3,1,0:T(8,128)(2,1)}, u32[]{:S(2)}, u32[]{:S(2)}) async-start(bf16[8,2,128,2,128]{4,2,3,1,0:T(8,128)(2,1)} %broadcast_select_fusion), calls=%async_computation | async-start | bytes 2097152 | tf_op jit(solution)/shard_map/all_to_all | solution.py:162
  28.0 2.4 reshape.866
  34.1 7.7 %fusion.181 = (f32[128,4,8]{2,1,0:T(4,128)}, f32[128,4,1,8,4]{3,4,1,0,2:T(4,128)}) fusion(bf16[128,4,8,128]{3,2,1,0:T(8,128)(2,1)} %reshape.866, bf16[128,4,2,128]{3,1,0,2:T(4,128)(2,1)S(1)} %bitcast.561, pred[4,4]{1,0:T(4,128)(4,1)S(1)} %iota_compare_fusion.3), kind=kOutput, calls=%fused_computation.287 | convolution fusion | flops 4239360 | bytes 1262080 | tf_op jit(solution)/shard_map/rtgqd,rugd->rtgqu/dot_general | solution.py:187
  42.0 5.3 %collective-permute-start = (bf16[8,2,128,2,128]{4,2,3,1,0:T(8,128)(2,1)}, bf16[8,2,128,2,128]{4,2,3,1,0:T(8,128)(2,1)}, u32[]{:S(2)}, u32[]{:S(2)}) collective-permute-start(bf16[8,2,128,2,128]{4,2,3,1,0:T(8,128)(2,1)} %all-to-all-done), channel_id=1, source_target_pairs={{0,128},{64,192},{128,0},{192,64},{1,129},{65,193},{129,1},{193,65... | collective-permute-start | bytes 3145736 | tf_op jit(solution)/shard_map/ppermute | solution.py:18
  47.9 2.1 gather_fusion.3
  53.2 3.9 %all-gather.3.cloned.1.call-done = bf16[1,2,1024,2,128]{4,2,3,1,0:T(8,128)(2,1)} async-done(((bf16[1,2,128,2,128]{4,2,3,1,0:T(8,128)(2,1)}), bf16[1,2,1024,2,128]{4,2,3,1,0:T(8,128)(2,1)}) %all-gather.3.cloned.1.call-update) | async-done | bytes 1048592 | tf_op jit(solution)/shard_map/all_gather | solution.py:120
  59.1 2.2 fusion.109
  61.3 14.7 %collective-permute-done = bf16[8,2,128,2,128]{4,2,3,1,0:T(8,128)(2,1)} collective-permute-done((bf16[8,2,128,2,128]{4,2,3,1,0:T(8,128)(2,1)}, bf16[8,2,128,2,128]{4,2,3,1,0:T(8,128)(2,1)}, u32[]{:S(2)}, u32[]{:S(2)}) %collective-permute-start) | collective-permute-done | bytes 1048608 | tf_op jit(solution)/shard_map/ppermute | solution.py:18
  76.1 4.0 %gather_fusion.1 = bf16[48,128,2,128]{3,1,2,0:T(8,128)(2,1)} fusion(bf16[8,2,128,2,128]{4,2,3,1,0:T(8,128)(2,1)} %collective-permute-done, s32[48]{0:T(128)S(1)} %fusion.163), kind=kCustom, calls=%fused_computation.1 | custom fusion | bytes 6291840 | tf_op jit(solution)/shard_map/gather | solution.py:176
  80.1 3.5 %bitcast_select_fusion.4 = bf16[48,128,2,128]{3,1,0,2:T(8,128)(2,1)S(1)} fusion(bf16[48,128,2,128]{3,1,2,0:T(8,128)(2,1)} %gather_fusion.1, bf16[1,48,128,2,128]{4,3,2,1,0:T(2,128)(2,1)} %param.21, pred[48]{0:T(512)(128)(4,1)S(1)} %copy-done.23), kind=kLoop, calls=%fused_computation.119 | loop fusion | flops 1572864 | bytes 9437232 | tf_op jit(solution)/shard_map/jit(_where)/select_n | solution.py:177
  83.5 1.7 copy-done.4
  89.6 2.3 fusion.103
  95.2 37.0 %pmax.7 = f32[128,4,1,8]{0,3,1,2:T(8,128)S(1)} all-reduce(f32[128,4,1,8]{0,3,1,2:T(8,128)S(1)} %bitcast.567), channel_id=1, replica_groups=mesh['section'=4,'mp'=8,'seq'=8] {'seq'}, use_global_device_ids=true, to_apply=%region_30.31 | all-reduce | flops 4096 | bytes 32768 | tf_op jit(solution)/shard_map/pmax | solution.py:273
  133.0 15.5 %psum.15 = bf16[128,4,1,8]{0,3,1,2:T(8,128)(2,1)S(1)} all-reduce(bf16[128,4,1,8]{0,3,1,2:T(8,128)(2,1)S(1)} %fusion.112), channel_id=1, replica_groups=mesh['section'=4,'mp'=8,'seq'=8] {'seq'}, use_global_device_ids=true, to_apply=%region_34.35 | all-reduce | flops 4096 | bytes 16384 | tf_op jit(solution)/shard_map/psum | solution.py:276
  149.4 3.0 %fusion.122 = f32[128,4,8]{2,1,0:T(4,128)} fusion(f32[128,4,1,8,4]{3,4,1,0,2:T(4,128)} %get-tuple-element.299, f32[128,4,8]{2,1,0:T(4,128)} %copy.182, pred[4,4]{1,0:T(4,128)(4,1)S(1)} %copy-done.26), kind=kLoop, calls=%fused_computation.172 | loop fusion | flops 45056 | bytes 98320 | tf_op jit(solution)/shard_map/reduce_sum | solution.py:198
  153.5 3.0 %fusion.97 = bf16[128,4,1,8,128]{4,0,3,1,2:T(8,128)(2,1)} fusion(f32[128,4,8]{0,2,1:T(8,128)S(1)} %get-tuple-element.279, f32[4,8,128,48]{2,1,0,3:T(8,128)S(1)} %bitcast.556, s32[48]{0:T(128)} %copy-done.24, pred[48]{0:T(512)(128)(4,1)S(1)} %copy-done.21), kind=kOutput, calls=%fused_computation.141 | convolution fusion | flops 303050752 | bytes 1851632 | tf_op jit(solution)/shard_map/dot_general | solution.py:263
  156.8 3.4 %fusion.127 = f32[128,4,8,128]{3,2,1,0:T(8,128)} fusion(f32[128,4,1,8,4]{3,4,1,0,2:T(4,128)} %get-tuple-element.299, f32[128,4,8]{2,1,0:T(4,128)} %copy.182, pred[4,4]{1,0:T(4,128)(4,1)S(1)} %copy-done.27, bf16[128,4,2,128]{3,1,0,2:T(4,128)(2,1)} %bitcast.562), kind=kOutput, calls=%fused_computation.177 | convolution fusion | flops 4243456 | bytes 3538960 | tf_op jit(solution)/shard_map/rtgqu,rugd->rtgqd/dot_general | solution.py:199
  160.2 63.2 %all-reduce.2.cloned.1.call-done = bf16[128,4,1,8,128]{4,0,3,1,2:T(8,128)(2,1)} async-done(((bf16[128,4,1,8,128]{4,0,3,1,2:T(8,128)(2,1)}), bf16[128,4,1,8,128]{4,0,3,1,2:T(8,128)(2,1)}) %all-reduce.2.cloned.1.call-update) | async-done | bytes 1048592 | tf_op jit(solution)/shard_map/psum | solution.py:277
  223.4 3.4 %fusion.83 = bf16[128,4,1,8,128]{4,0,3,1,2:T(8,128)(2,1)} fusion(f32[128,4,8,128]{3,2,1,0:T(8,128)} %fusion.127, bf16[128,4,1,8,128]{4,0,3,1,2:T(8,128)(2,1)} %all-reduce.2.cloned.1.call-done, f32[128,4,8]{0,2,1:T(8,128)S(1)} %get-tuple-element.278, f32[128,4,8]{0,2,1:T(8,128)S(1)} %get-tuple-element.277), kind=kLoop, calls=%fused_computation.122 | loop fusion | flops 2621440 | bytes 4227072 | tf_op jit(solution)/shard_map/convert_element_type | solution.py:205
  226.8 2.3 copy.186
  229.1 3.5 %fusion.94 = bf16[128,4,1024]{2,0,1:T(8,128)(2,1)} fusion(bf16[128,4,1024]{0,2,1:T(8,128)(2,1)} %bitcast.559, bf16[1,1024,1024]{2,1,0:T(8,128)(2,1)S(1)} %copy-done), kind=kOutput, calls=%fused_computation.140 | convolution fusion | flops 1074266112 | bytes 4194304 | tf_op jit(solution)/shard_map/dot_general | solution.py:286
  232.6 2.2 fusion.177
  237.2 2.5 conditional.7
  239.6 2.2 conditional.5
  242.6 2.9 %conditional.4 = (f32[64,1,8]{0,2,1:T(8,128)S(1)}, f32[64,1,8,128]{3,0,2,1:T(8,128)}) conditional(s32[]{:T(128)} %bitcast.58, () %tuple.38, (s32[1024]{0:T(1024)S(1)}, s32[2,64]{1,0:T(2,128)S(1)}, bf16[2,1024,1,128]{3,1,2,0:T(8,128)(2,1)S(1)}, bf16[2,2,64,1,8,128]{5,4,2,1,0,3:T(8,128)(2,1)S(1)}, bf16[2,1024,1,128]{3,1,2,0:T(8,128)(2,1)}) %tuple.131), branch_computations={%region_1.2_spmd, %region_2.5_spmd} | conditional | flops 275383808 | bytes 10648364 | solution.py:103
  245.5 4.1 %conditional.6 = ((f32[64,1,8]{0,2,1:T(8,128)S(1)}, f32[64,1,8,128]{3,0,2,1:T(8,128)})) conditional(s32[]{:T(128)} %bitcast.58, (f32[64,1,8]{0,2,1:T(8,128)S(1)}, f32[64,1,8,128]{3,0,2,1:T(8,128)}) %tuple.41, (s32[1024]{0:T(1024)S(1)}, s32[2,64]{1,0:T(2,128)S(1)}, bf16[2,1024,1,128]{3,1,2,0:T(8,128)(2,1)S(1)}, ...), branch_computations={%region_11.12_spmd, %region_12.15_spmd} | conditional | flops 275449856 | bytes 10916660 | solution.py:103
  246.6 2.4 fusion.43
  253.5 17.5 %reduce-scatter.2.cloned.1.call-done = bf16[16,4,1024]{2,0,1:T(8,128)(2,1)} async-done(((bf16[128,4,1024]{2,0,1:T(8,128)(2,1)}), bf16[16,4,1024]{2,0,1:T(8,128)(2,1)}) %reduce-scatter.2.cloned.1.call-update) | async-done | bytes 131088 | tf_op jit(solution)/shard_map/reduce_scatter | solution.py:287
  271.0 1.7 copy.188
  (170 shorter events, 38.8 us)
Async XLA Ops:
  7.2 221.9 %copy-start = (bf16[1,1024,1024]{2,1,0:T(8,128)(2,1)S(1)}, bf16[1,1024,1024]{2,1,0:T(8,128)(2,1)}, u32[]{:S(2)}) copy-start(bf16[1,1024,1024]{2,1,0:T(8,128)(2,1)} %param.22) | copy-start | bytes 6291460
  16.9 9.9 %copy-start.2 = (bf16[1,2,128,2,128]{4,3,2,1,0:T(2,128)(2,1)S(1)}, bf16[1,2,128,2,128]{4,3,2,1,0:T(2,128)(2,1)}, u32[]{:S(2)}) copy-start(bf16[1,2,128,2,128]{4,3,2,1,0:T(2,128)(2,1)} %param.18) | copy-start | bytes 393220
  16.9 10.9 %copy-start.28 = (s32[48]{0:T(128)S(1)}, s32[48]{0:T(128)}, u32[]{:S(2)}) copy-start(s32[48]{0:T(128)} %param.23) | copy-start | bytes 580
  16.9 11.0 %copy-start.15 = (bf16[1,128,4,2,128]{4,3,2,1,0:T(2,128)(2,1)S(1)}, bf16[1,128,4,2,128]{4,3,2,1,0:T(2,128)(2,1)}, u32[]{:S(2)}) copy-start(bf16[1,128,4,2,128]{4,3,2,1,0:T(2,128)(2,1)} %param.20) | copy-start | bytes 786436
  19.3 11.0 %copy-start.9 = (bf16[1,2,128,1024]{3,2,1,0:T(8,128)(2,1)S(1)}, bf16[1,2,128,1024]{3,2,1,0:T(8,128)(2,1)}, u32[]{:S(2)}) copy-start(bf16[1,2,128,1024]{3,2,1,0:T(8,128)(2,1)} %param.17) | copy-start | bytes 1572868
  19.3 22.7 %all-to-all-start = ((bf16[8,2,128,2,128]{4,2,3,1,0:T(8,128)(2,1)}), bf16[8,2,128,2,128]{4,2,3,1,0:T(8,128)(2,1)}, u32[]{:S(2)}, u32[]{:S(2)}) async-start(bf16[8,2,128,2,128]{4,2,3,1,0:T(8,128)(2,1)} %broadcast_select_fusion), calls=%async_computation | async-start | bytes 2097152 | tf_op jit(solution)/shard_map/all_to_all | solution.py:162
  26.8 3.6 %copy-start.1 = (s32[128]{0:T(128)S(1)}, s32[128]{0:T(128)}, u32[]{:S(2)}) copy-start(s32[128]{0:T(128)} %param.25) | copy-start | bytes 1540
  26.8 30.3 %all-gather.3.cloned.1.call-start = ((), (), s32[]{:S(2)}) async-start(), calls=%async_computation.4 | async-start | bytes 1179648 | tf_op jit(solution)/shard_map/all_gather | solution.py:120
  27.5 195.8 %all-reduce.2.cloned.1.call-start = ((), (), s32[]{:S(2)}) async-start(), calls=%async_computation.2 | async-start | bytes 2097152 | tf_op jit(solution)/shard_map/psum | solution.py:277
  27.7 2.6 copy-start.22
  27.8 4.9 %copy-start.20 = (pred[48]{0:T(512)(128)(4,1)}, pred[48]{0:T(512)(128)(4,1)S(1)}, u32[]{:S(2)}) copy-start(pred[48]{0:T(512)(128)(4,1)S(1)} %get-tuple-element.251) | copy-start | bytes 148
  27.9 4.9 %copy-start.24 = (s32[48]{0:T(128)}, s32[48]{0:T(128)S(1)}, u32[]{:S(2)}) copy-start(s32[48]{0:T(128)S(1)} %get-tuple-element.254) | copy-start | bytes 580
  28.0 6.1 %copy-start.8 = (bf16[1,128,4,2,128]{4,2,1,3,0:T(4,128)(2,1)}, bf16[1,128,4,2,128]{4,2,1,3,0:T(4,128)(2,1)S(1)}, u32[]{:S(2)}) copy-start(bf16[1,128,4,2,128]{4,2,1,3,0:T(4,128)(2,1)S(1)} %copy.213) | copy-start | bytes 786436
  30.5 17.5 %copy-start.19 = (s32[1024]{0:T(1024)}, s32[1024]{0:T(1024)S(1)}, u32[]{:S(2)}) copy-start(s32[1024]{0:T(1024)S(1)} %pad_clamp_fusion) | copy-start | bytes 12292
  31.4 16.6 %copy-start.25 = (pred[4,4]{1,0:T(4,128)(4,1)}, pred[4,4]{1,0:T(4,128)(4,1)S(1)}, u32[]{:S(2)}) copy-start(pred[4,4]{1,0:T(4,128)(4,1)S(1)} %iota_compare_fusion.3) | copy-start | bytes 52
  42.0 34.0 %collective-permute-start = (bf16[8,2,128,2,128]{4,2,3,1,0:T(8,128)(2,1)}, bf16[8,2,128,2,128]{4,2,3,1,0:T(8,128)(2,1)}, u32[]{:S(2)}, u32[]{:S(2)}) collective-permute-start(bf16[8,2,128,2,128]{4,2,3,1,0:T(8,128)(2,1)} %all-to-all-done), channel_id=1, source_target_pairs={{0,128},{64,192},{128,0},{192,64},{1,129},{65,193},{129,1},{193,65... | collective-permute-start | bytes 3145736 | tf_op jit(solution)/shard_map/ppermute | solution.py:18
  61.3 18.8 %copy-start.23 = (pred[48]{0:T(512)(128)(4,1)S(1)}, pred[48]{0:T(512)(128)(4,1)}, u32[]{:S(2)}) copy-start(pred[48]{0:T(512)(128)(4,1)} %copy-done.22) | copy-start | bytes 148
  80.1 5.1 %copy-start.17 = (pred[48,128]{1,0:T(8,128)(4,1)S(1)}, pred[48,128]{1,0:T(8,128)(4,1)}, u32[]{:S(2)}) copy-start(pred[48,128]{1,0:T(8,128)(4,1)} %iota_compare_fusion) | copy-start | bytes 18436
  83.5 1.7 copy-start.4
  85.2 2.6 copy-start.18
  91.9 40.3 %copy-start.21 = (pred[48]{0:T(512)(128)(4,1)S(1)}, pred[48]{0:T(512)(128)(4,1)}, u32[]{:S(2)}) copy-start(pred[48]{0:T(512)(128)(4,1)} %copy-done.20) | copy-start | bytes 148
  91.9 56.7 %copy-start.16 = (f32[128,4,8]{0,2,1:T(8,128)S(1)}, f32[128,4,8]{0,2,1:T(8,128)}, u32[]{:S(2)}) copy-start(f32[128,4,8]{0,2,1:T(8,128)} %copy.181) | copy-start | bytes 49156
  92.9 56.5 %copy-start.26 = (pred[4,4]{1,0:T(4,128)(4,1)S(1)}, pred[4,4]{1,0:T(4,128)(4,1)}, u32[]{:S(2)}) copy-start(pred[4,4]{1,0:T(4,128)(4,1)} %copy-done.25) | copy-start | bytes 52
  149.4 7.4 %copy-start.27 = (pred[4,4]{1,0:T(4,128)(4,1)S(1)}, pred[4,4]{1,0:T(4,128)(4,1)}, u32[]{:S(2)}) copy-start(pred[4,4]{1,0:T(4,128)(4,1)} %copy-done.25) | copy-start | bytes 52
  156.5 114.4 %reduce-scatter.2.cloned.1.call-start = ((), (), s32[]{:S(2)}) async-start(), calls=%async_computation.3 | async-start | bytes 1179648 | tf_op jit(solution)/shard_map/reduce_scatter | solution.py:287
  232.6 2.2 copy-start.10
  232.6 2.2 copy-start.3
  235.3 1.8 copy-start.5
  235.3 1.8 copy-start.29
  239.9 1.3 copy-start.12
  242.9 1.3 copy-start.13
  245.5 1.0 copy-start.14
  (3 other events, 2.7 us)
Sparse Core Ops, SparseCore 0:
  29.5 27.5 all-gather.2
  156.7 66.6 all-reduce.1
  232.7 38.2 reduce-scatter.1
where the time goes:
time: 284 us; the launch traced here: 279 us
  waiting for transfers between devices  99.6 us (35%)
  blocking collectives  52.5 us (18%)
  local copies, waits for them, and re-layouts  38.9 us (14%)
  matrix products  34.5 us (12%)
  other arithmetic  24.9 us (9%)
  between operations  15.5 us (5%)
  starting transfers between devices  13.1 us (5%)
    psum x1, waiting for transfers between devices, decode_group(): lax.psum((local_acc * shrink[..., None]).astype(jnp.bfloat16), 'seq')  63.2 us
    pmax x1, blocking collectives, decode_group(): top_max = lax.pmax(local_max, 'seq')  37 us
    reduce_scatter x1, waiting for transfers between devices, decode_group(): lax.psum_scatter(product.reshape(lax.axis_size('mp') * share_rows, step_c...  17.5 us
    psum x1, blocking collectives, decode_group(): lax.psum((local_sum * shrink).astype(jnp.bfloat16), 'seq')  15.5 us
    ppermute x1, waiting for transfers between devices, passed_along(): return lax.ppermute(x, axis, [(i, (i + by) % peers) for i in range(peers)])  14.7 us
    dot_general x6, matrix products, absorb_block(): jnp.einsum('igqj,jgd->igqd', attention_weight.astype(jnp.bfloat16), value...  8.61 us
    dot_general x1, matrix products, finish_rows(): jnp.einsum('rtgqd,rugd->rtgqu', reshaped_input, incoming_keys, preferred_...  7.69 us
    all_to_all x1, starting transfers between devices, deliver_pages(): lax.all_to_all(outgoing, 'seq', split_axis=0, concat_axis=0, tiled=True)  7.48 us
  transfers between devices with their start and end apart: 5, of which 5 were waited for; matrix products, arithmetic and copies ran while one was open for 17% of the time, Pallas kernels for 0%

commit v1 on v0

v1 whole, which is shorter than its diff:
```python
import functools
import math

import jax
import jax.numpy as jnp
from jax import lax
from jax.experimental import pallas as pl
from jax.experimental.pallas import tpu as pltpu
from jax.sharding import PartitionSpec as P

HEAD = 128
PAGE = 128
MAXP = 1024
BLOCKS = 2
NEG = -1e30
F32 = jnp.float32
BF16 = jnp.bfloat16
MESH = pl.DeviceIdType.MESH
SCALE = 1.0 / (math.sqrt(HEAD) * math.log(2.0))


def dot_nt(a, b):
    return lax.dot_general(a, b, (((1,), (1,)), ((), ())), preferred_element_type=F32)


def dot_nn(a, b, precision=None):
    return lax.dot_general(
        a, b, (((1,), (0,)), ((), ())), preferred_element_type=F32, precision=precision
    )


def iota(shape, dim):
    return lax.broadcasted_iota(jnp.int32, shape, dim)


def kernel(
    nsec, nseq, nmp, slots, rows, heads, steps,
    pq_h, pp_h, dq_h, dp_h, pool_h, w_h, slot_s, ctx_s,
    pre_h, mix_o,
    pq_v, pp_v, dq_v, dp_v, pool_v, w_v, kv, q0, r0_out, r0_in, lse, accs,
    part, part_in, att, prod, prod_in, pre_v,
    in_sem, out_sem, kv_s, kv_r, z_s, z_r, lse_s, lse_r, rs_s, rs_r, ag_s, ag_r, mp_s, mp_r,
):
    hs = heads * steps
    own = rows // nseq
    me = lax.axis_index("seq")
    mp = lax.axis_index("mp")
    sec = lax.axis_index("section")
    partner = {"section": lax.rem(sec + nsec // 2, nsec)}

    def seq_dev(k):
        return {"seq": lax.rem(me + k, nseq)}

    def mp_dev(k):
        return {"mp": lax.rem(mp + k, nmp)}

    def remote(src, dst, send, recv, device):
        return pltpu.make_async_remote_copy(
            src_ref=src, dst_ref=dst, send_sem=send, recv_sem=recv,
            device_id=device, device_id_type=MESH,
        )

    chunk = slots // 4 * 2 * PAGE
    loads = [
        pltpu.make_async_copy(pp_h, pp_v, in_sem.at[0]),
        pltpu.make_async_copy(dq_h, dq_v, in_sem.at[1]),
        pltpu.make_async_copy(dp_h.at[pl.ds(me * own * 2 * steps, own * 2 * steps)], dp_v, in_sem.at[2]),
        pltpu.make_async_copy(pool_h, pool_v, in_sem.at[3]),
        pltpu.make_async_copy(pq_h, pq_v, in_sem.at[4]),
        pltpu.make_async_copy(w_h, w_v, in_sem.at[5]),
    ]
    for c in loads:
        c.start()

    barrier = pltpu.get_barrier_semaphore()
    for k in range(1, nseq):
        pl.semaphore_signal(barrier, inc=1, device_id=seq_dev(k), device_id_type=MESH)
    for k in range(1, nmp):
        pl.semaphore_signal(barrier, inc=1, device_id=mp_dev(k), device_id_type=MESH)
    pl.semaphore_signal(barrier, inc=1, device_id=partner, device_id_type=MESH)

    loads[0].wait()
    ri = iota((2 * PAGE, 2 * PAGE), 0)
    ci = iota((2 * PAGE, 2 * PAGE), 1)
    pick = jnp.where(ci == jnp.where(ri < PAGE, 2 * ri, 2 * (ri - PAGE) + 1), 1.0, 0.0).astype(BF16)
    for b in range(BLOCKS):
        both = dot_nn(pick, pp_v[b * 2 * PAGE:(b + 1) * 2 * PAGE, :]).astype(BF16)
        kv[me, b * PAGE:(b + 1) * PAGE, :] = both[:PAGE]
        kv[me, (BLOCKS + b) * PAGE:(BLOCKS + b + 1) * PAGE, :] = both[PAGE:]
    loads[1].wait()

    pl.semaphore_wait(barrier, nseq + nmp - 1)

    q_out = remote(dq_v.at[0], q0, z_s.at[0], z_r.at[0], partner)
    q_out.start()
    kv_copies = [
        remote(kv.at[me], kv.at[me], kv_s.at[k - 1], kv_r.at[k - 1], seq_dev(k))
        for k in range(1, nseq)
    ]
    for c in kv_copies:
        c.start()

    lane = iota((hs, 128), 1)
    lane1 = iota((8, 128), 1)
    key_lane = iota((hs, 2 * PAGE), 1)
    key_id = jnp.where(key_lane % 2 == 0, key_lane // 2, PAGE)

    def merge(state, index, row, m, l):
        top, total, slot_top, slot_row = state
        hit = lane == row
        fresh = jnp.where(hit, jnp.maximum(top, m), top)
        total = total * jnp.exp2((top - fresh) * SCALE) + jnp.where(
            hit, l * jnp.exp2((m - fresh) * SCALE), 0.0
        )
        slot_top = jnp.where(lane == index, m, slot_top)
        slot_row = jnp.where(lane1 == index, row, slot_row)
        return fresh, total, slot_top, slot_row

    def slot_group(g, state, width):
        done = []
        for i in range(width):
            j = g * width + i
            entry = slot_s[j]
            live = entry >= 0
            row = jnp.where(live, entry // MAXP, 0)
            count = jnp.where(live, jnp.clip(ctx_s[row] - (entry % MAXP) * PAGE, 0, PAGE), 0)
            page = pool_v[pl.ds(pl.multiple_of(j * 2 * PAGE, 2 * PAGE), 2 * PAGE), :]
            done.append((j, jnp.where(live, row, -1), count, page, dot_nt(dq_v[row], page)))
        for j, row, count, page, scores in done:
            allowed = key_id < count
            scores = jnp.where(allowed, scores, NEG)
            m = jnp.max(scores, axis=1, keepdims=True)
            p = jnp.where(allowed, jnp.exp2((scores - m) * SCALE), 0.0)
            l = jnp.sum(p, axis=1, keepdims=True)
            acc = dot_nn(pltpu.roll(p, 1, 1).astype(BF16), page)
            accs[pl.ds(pl.multiple_of(j * hs, hs), hs), :] = acc
            state = merge(state, j, row, m, l)
        return state

    state = (
        jnp.full((hs, 128), NEG, F32), jnp.zeros((hs, 128), F32),
        jnp.full((hs, 128), NEG, F32), jnp.full((8, 128), -1, jnp.int32),
    )
    width = 4
    loads[3].wait()
    first = slots // width // 2
    state = lax.fori_loop(0, first, lambda g, s: slot_group(g, s, width), state)

    q_out.wait()
    k_mine = kv[me, 0:BLOCKS * PAGE, :]
    v_mine = kv[me, BLOCKS * PAGE:2 * BLOCKS * PAGE, :]
    scores = dot_nt(q0[...], k_mine)
    place = iota((hs, BLOCKS * PAGE), 1)
    position = jnp.where(place < PAGE, place, place - PAGE + nseq * PAGE) + me * PAGE
    allowed = position < ctx_s[0]
    scores = jnp.where(allowed, scores, NEG)
    m = jnp.max(scores, axis=1, keepdims=True)
    p = jnp.where(allowed, jnp.exp2((scores - m) * SCALE), 0.0)
    l = jnp.sum(p, axis=1, keepdims=True)
    r0_out[0:hs, :] = dot_nn(p.astype(BF16), v_mine)
    r0_out[hs:2 * hs, :] = jnp.where(lane == 0, m, l)
    r0_copy = remote(r0_out, r0_in, z_s.at[1], z_r.at[1], partner)
    r0_copy.start()

    state = lax.fori_loop(first, slots // width, lambda g, s: slot_group(g, s, width), state)

    loads[2].wait()
    recent = dp_v[...]
    rq = dq_v[pl.ds(me * own, own)].reshape(own * hs, HEAD)
    scores = dot_nt(rq, recent)
    ri = iota(scores.shape, 0)
    ci = iota(scores.shape, 1)
    allowed = (
        (ci % 2 == 0) & (ci // (2 * steps) == ri // hs) & ((ci % (2 * steps)) // 2 <= ri % steps)
    )
    scores = jnp.where(allowed, scores, NEG)
    m = jnp.max(scores, axis=1, keepdims=True)
    p = jnp.where(allowed, jnp.exp2((scores - m) * SCALE), 0.0)
    l = jnp.sum(p, axis=1, keepdims=True)
    accs[slots * hs:(slots + own) * hs, :] = dot_nn(pltpu.roll(p, 1, 1).astype(BF16), recent)
    for r in range(own):
        state = merge(
            state, slots + r, me * own + r, m[r * hs:(r + 1) * hs], l[r * hs:(r + 1) * hs]
        )

    r0_copy.wait()
    stats = r0_in[hs:2 * hs, :]
    row0 = slots + own
    accs[row0 * hs:(row0 + 1) * hs, :] = r0_in[0:hs, :]
    state = merge(state, row0, 0, stats[:, 0:1], stats[:, 1:2])
    pad_rows = accs.shape[0] - (row0 + 1) * hs
    accs[(row0 + 1) * hs:, :] = jnp.zeros((pad_rows, HEAD), F32)

    top, total, slot_top, slot_row = state
    lse[me] = jnp.where(
        total > 0.0, top * SCALE + jnp.log2(jnp.maximum(total, 1e-30)), NEG
    )
    lse_copies = [
        remote(lse.at[me], lse.at[me], lse_s.at[k - 1], lse_r.at[k - 1], seq_dev(k))
        for k in range(1, nseq)
    ]
    for c in lse_copies:
        c.start()

    loads[4].wait()
    kv_ready = []

    def prompt_piece(b, pair):
        two = pq_v[b, :, pl.ds(pl.multiple_of(pair * 2 * HEAD, 2 * HEAD), 2 * HEAD)]
        q = jnp.concatenate([two[:, :HEAD], two[:, HEAD:]], axis=0)
        n = nseq * PAGE
        k_own = kv[:, b * PAGE:(b + 1) * PAGE, :].reshape(n, HEAD)
        v_own = kv[:, (BLOCKS + b) * PAGE:(BLOCKS + b + 1) * PAGE, :].reshape(n, HEAD)
        s_own = dot_nt(q, k_own)
        limit = me * PAGE + iota((2 * PAGE, n), 0) % PAGE
        s_own = jnp.where(iota((2 * PAGE, n), 1) <= limit, s_own, NEG)
        m = jnp.max(s_own, axis=1, keepdims=True)
        if b:
            k_old = kv[:, 0:PAGE, :].reshape(n, HEAD)
            v_old = kv[:, BLOCKS * PAGE:(BLOCKS + 1) * PAGE, :].reshape(n, HEAD)
            s_old = dot_nt(q, k_old)
            m = jnp.maximum(m, jnp.max(s_old, axis=1, keepdims=True))
        p = jnp.exp2((s_own - m) * SCALE)
        l = jnp.sum(p, axis=1, keepdims=True)
        o = dot_nn(p.astype(BF16), v_own)
        if b:
            p = jnp.exp2((s_old - m) * SCALE)
            l = l + jnp.sum(p, axis=1, keepdims=True)
            o = o + dot_nn(p.astype(BF16), v_old)
        o = (o / l).astype(BF16)
        pre_v[b, :, pl.ds(pl.multiple_of(pair * 2 * HEAD, 2 * HEAD), 2 * HEAD)] = jnp.concatenate(
            [o[:PAGE], o[PAGE:]], axis=1
        )

    def prompt_pieces(b, lo, hi):
        def step(i, carry):
            prompt_piece(b, i)
            return carry

        lax.fori_loop(lo, hi, step, 0)

    for c in kv_copies:
        c.wait()
    pairs = heads // 2
    prompt_pieces(0, 0, pairs)

    for c in lse_copies:
        c.wait()
    every = [lse[k] for k in range(nseq)]
    peak = functools.reduce(jnp.maximum, every)
    whole = peak + jnp.log2(sum(jnp.exp2(e - peak) for e in every))
    row_pick = jnp.where(
        iota((128, 128), 0) == jnp.broadcast_to(slot_row[0:1], (128, 128)), 1.0, 0.0
    )
    whole_slot = dot_nn(whole, row_pick, lax.Precision.HIGHEST)
    factor = jnp.exp2(slot_top * SCALE - whole_slot)
    count = accs.shape[0] // hs
    for i in range(hs):
        weights = (row_pick * jnp.broadcast_to(factor[i:i + 1], (128, 128)))[:rows, :count]
        sums = dot_nn(
            weights.astype(BF16), accs[pl.ds(i, count, stride=hs), :].astype(BF16)
        ).astype(BF16)
        for s in range(nseq):
            part[s, i] = sums[s * own:(s + 1) * own]

    rs_copies = [
        remote(
            part.at[lax.rem(me + k, nseq)], part_in.at[k - 1],
            rs_s.at[k - 1], rs_r.at[k - 1], seq_dev(k),
        )
        for k in range(1, nseq)
    ]
    for c in rs_copies:
        c.start()

    prompt_pieces(1, 0, pairs // 2)

    for c in rs_copies:
        c.wait()
    for i in range(heads):
        sl = slice(i * steps, (i + 1) * steps)
        tot = part[me, sl].astype(F32)
        for k in range(nseq - 1):
            tot = tot + part_in[k, sl].astype(F32)
        att[me, sl] = tot.astype(BF16)

    ag_copies = [
        remote(att.at[me], att.at[me], ag_s.at[k - 1], ag_r.at[k - 1], seq_dev(k))
        for k in range(1, nseq)
    ]
    for c in ag_copies:
        c.start()

    prompt_pieces(1, pairs // 2, pairs)
    pre_copy = pltpu.make_async_copy(pre_v, pre_h, out_sem)
    pre_copy.start()

    for c in ag_copies:
        c.wait()
    loads[5].wait()

    def slab_product(s):
        left = jnp.concatenate(
            [att[s, h * steps:(h + 1) * steps].reshape(steps * own, HEAD) for h in range(heads)],
            axis=1,
        )
        return dot_nn(left, w_v[...])

    mp_copies = []
    for k in range(1, nmp):
        prod[k] = slab_product(lax.rem(mp + k, nmp)).astype(BF16)
        c = remote(prod.at[k], prod_in.at[k - 1], mp_s.at[k - 1], mp_r.at[k - 1], mp_dev(k))
        c.start()
        mp_copies.append(c)
    mix = slab_product(mp)
    for k, c in enumerate(mp_copies):
        c.wait()
        mix = mix + prod_in[k].astype(F32)
    mix_o[...] = mix.astype(BF16)
    pre_copy.wait()


def body(
    prompt_queries, prompt_pairs, decode_queries, decode_pairs, cache_pool, out_weight,
    slot_pages, placement, context_len,
):
    nsec, nseq, nmp = (lax.axis_size(a) for a in ("section", "seq", "mp"))
    _, blocks, btok, qwidth = prompt_queries.shape
    _, rows, steps, _ = decode_queries.shape
    slots = cache_pool.shape[1]
    width = out_weight.shape[2]
    heads = qwidth // HEAD
    hs = heads * steps
    own = rows // nseq
    pq = prompt_queries[0]
    pp = prompt_pairs.reshape(blocks * btok * 2, HEAD)
    dq = decode_queries.reshape(rows, steps, heads, HEAD).transpose(0, 2, 1, 3).reshape(rows, hs, HEAD)
    dp = decode_pairs.reshape(rows * steps * 2, HEAD)
    pool = cache_pool.reshape(slots * PAGE * 2, HEAD)
    w = out_weight[0]
    count = -(-(slots + own + 1) // 16) * 16
    any_spec = pl.BlockSpec(memory_space=pl.ANY)
    smem_spec = pl.BlockSpec(memory_space=pltpu.SMEM)
    dma = pltpu.SemaphoreType.DMA
    prefill, mixed = pl.pallas_call(
        functools.partial(kernel, nsec, nseq, nmp, slots, rows, heads, steps),
        out_shape=(
            jax.ShapeDtypeStruct(pq.shape, BF16),
            jax.ShapeDtypeStruct((steps * own, width), BF16),
        ),
        in_specs=[any_spec] * 6 + [smem_spec] * 2,
        out_specs=(any_spec, pl.BlockSpec(memory_space=pltpu.VMEM)),
        scratch_shapes=[
            pltpu.VMEM(pq.shape, BF16),
            pltpu.VMEM(pp.shape, BF16),
            pltpu.VMEM(dq.shape, BF16),
            pltpu.VMEM((own * 2 * steps, HEAD), BF16),
            pltpu.VMEM(pool.shape, BF16),
            pltpu.VMEM(w.shape, BF16),
            pltpu.VMEM((nseq,) + pp.shape, BF16),
            pltpu.VMEM((hs, HEAD), BF16),
            pltpu.VMEM((2 * hs, HEAD), F32),
            pltpu.VMEM((2 * hs, HEAD), F32),
            pltpu.VMEM((nseq, hs, 128), F32),
            pltpu.VMEM((count * hs, HEAD), F32),
            pltpu.VMEM((nseq, hs, own, HEAD), BF16),
            pltpu.VMEM((nseq, hs, own, HEAD), BF16),
            pltpu.VMEM((nseq, hs, own, HEAD), BF16),
            pltpu.VMEM((nmp, steps * own, width), BF16),
            pltpu.VMEM((nmp, steps * own, width), BF16),
            pltpu.VMEM(pq.shape, BF16),
            dma((6,)),
            dma,
            dma((nseq,)), dma((nseq,)),
            dma((2,)), dma((2,)),
            dma((nseq,)), dma((nseq,)),
            dma((nseq,)), dma((nseq,)),
            dma((nseq,)), dma((nseq,)),
            dma((nmp,)), dma((nmp,)),
        ],
        compiler_params=pltpu.CompilerParams(
            collective_id=0, has_side_effects=True, vmem_limit_bytes=56 * 1024 * 1024
        ),
    )(pq, pp, dq, dp, pool, w, slot_pages, context_len)
    mixed = mixed.reshape(steps, own, width).transpose(1, 0, 2)
    return prefill[None], mixed[None]


def solution(mesh):
    return jax.shard_map(
        body,
        mesh=mesh,
        in_specs=(
            P("section", None, "seq", "mp"),
            P("section", None, "seq", None, "mp"),
            P("section", None, None, "mp"),
            P("section", None, None, None, "mp"),
            P("section", "seq", None, None, "mp"),
            P("section", "mp", "seq"),
            P("seq"),
            P(),
            P(),
        ),
        out_specs=(P("section", None, "seq", "mp"), P("section", "mp", None, "seq")),
        check_vma=False,
    )
```

time: 284 us -> 74.6 us (0.26); the launches traced: 279 us -> 74.5 us
  waiting for transfers between devices: 99.6 us -> 0 us
  Pallas kernels: 0 us -> 70.3 us
  blocking collectives: 52.5 us -> 0 us
  local copies, waits for them, and re-layouts: 38.9 us -> 3.53 us
  matrix products: 34.5 us -> 0 us
  other arithmetic: 24.9 us -> 0 us
  between operations: 15.5 us -> 0.64 us
  starting transfers between devices: 13.1 us -> 0 us
    pallas_call x0 -> x1, Pallas kernels: none -> 70.3 us  [body(): pl.pallas_call(functools.partial(kernel, nsec, nseq, nmp, slots, rows, he...]
    psum x1 -> x0, waiting for transfers between devices: 63.2 us -> none  [decode_group(): lax.psum((local_acc * shrink[..., None]).astype(jnp.bfloat16), 'seq')]
    pmax x1 -> x0, blocking collectives: 37 us -> none  [decode_group(): top_max = lax.pmax(local_max, 'seq')]
    dot_general x19 -> x0, matrix products: 34.5 us -> none  [the longest x6 8.61 us: absorb_block(): jnp.einsum('igqj,jgd->igqd', attention_weight.astype(jnp.bfloat16), value...]
    reduce_scatter x1 -> x0, waiting for transfers between devices: 17.5 us -> none  [decode_group(): lax.psum_scatter(product.reshape(lax.axis_size('mp') * share_rows, step_c...]
    psum x1 -> x0, blocking collectives: 15.5 us -> none  [decode_group(): lax.psum((local_sum * shrink).astype(jnp.bfloat16), 'seq')]
    ppermute x1 -> x0, waiting for transfers between devices: 14.7 us -> none  [passed_along(): return lax.ppermute(x, axis, [(i, (i + by) % peers) for i in range(peers)])]
    gather x6 -> x0, local copies, waits for them, and re-layouts: 14.7 us -> none  [the longest x2 7 us: deliver_pages(): key_value_pairs[source_page]]
  transfers between devices with their start and end apart: 5 -> 0, of which waited for: 5 -> 0; matrix products, arithmetic and copies ran while one was open for 17% -> 0% of each run, Pallas kernels for 0% -> 0%
where the time goes in v1:
time: 74.6 us; the launch traced here: 74.5 us
  Pallas kernels  70.3 us (94%)
  local copies, waits for them, and re-layouts  3.53 us (5%)
    pallas_call x1, Pallas kernels, body(): pl.pallas_call(functools.partial(kernel, nsec, nseq, nmp, slots, rows, he...  70.3 us
    unnamed x1, local copies, waits for them, and re-layouts  1.87 us
    reshape x1, local copies, waits for them, and re-layouts, body(): mixed = mixed.reshape(steps, own, width).transpose(1, 0, 2)  1.66 us

profile of v1, /device:TPU:1, one launch (start us, length us, event | category | flops | bytes accessed | tf_op | source)
XLA Modules:
  0.0 74.5 jit_solution(3453843215821489499)
XLA Ops:
  0.6 70.3 %shard_map.95 = (bf16[2,128,1024]{2,1,0:T(8,128)(2,1)}, bf16[64,1024]{1,0:T(8,128)(2,1)}) custom-call(bf16[2,128,1024]{2,1,0:T(8,128)(2,1)} %bitcast.21, bf16[512,128]{1,0:T(8,128)(2,1)} %bitcast.23, bf16[128,32,128]{2,1,0:T(8,128)(2,1)} %bitcast.19, bf16[1024,128]{1,0:T(8,128)(2,1)} %bitcast.22, bf16[12288,128]{1,0:T(8,128)(2,1)} %bitcast.17, ...), custom_call_target="tpu_custom_call" | custom-call | tf_op jit(solution)/shard_map/pallas_call | solution.py:345
  70.9 1.7 %copy.13 = bf16[4,16,1024]{2,0,1:T(4,128)(2,1)} copy(bf16[4,16,1024]{2,1,0:T(8,128)(2,1)} %bitcast.25) | data formatting | bytes 262144 | tf_op jit(solution)/shard_map/reshape | solution.py:385
  72.6 1.9 %copy.15 = bf16[1,2,128,1024]{3,2,1,0:T(8,128)(2,1)} copy(bf16[1,2,128,1024]{3,2,1,0:T(8,128)(2,1)} %bitcast.20) | data formatting | bytes 1048576

commit v2 on v1

v2 whole, which is shorter than its diff:
```python
import functools
import math

import jax
import jax.numpy as jnp
from jax import lax
from jax.experimental import pallas as pl
from jax.experimental.pallas import tpu as pltpu
from jax.sharding import PartitionSpec as P

HEAD = 128
PAGE = 128
MAXP = 1024
BLOCKS = 2
NEG = -1e30
F32 = jnp.float32
BF16 = jnp.bfloat16
MESH = pl.DeviceIdType.MESH
SCALE = 1.0 / (math.sqrt(HEAD) * math.log(2.0))


def dot_nt(a, b):
    return lax.dot_general(a, b, (((1,), (1,)), ((), ())), preferred_element_type=F32)


def dot_nn(a, b, precision=None):
    return lax.dot_general(
        a, b, (((1,), (0,)), ((), ())), preferred_element_type=F32, precision=precision
    )


def iota(shape, dim):
    return lax.broadcasted_iota(jnp.int32, shape, dim)


def kernel(
    nsec, nseq, nmp, slots, rows, heads, steps,
    pq_h, pp_h, dq_h, dp_h, pool_h, w_h, slot_s, ctx_s,
    pre_h, mix_o,
    pq_v, pp_v, dq_v, dp_v, pool_v, w_v, kv, q0, r0_out, r0_in, lse_out, lse_in, lse_t, lse_t_in,
    accs, part, sib_in, part_in, att_f, att, prod, prod_in, mix_v, pre_v,
    in_sem, out_sem, kv_s, kv_r, z_s, z_r, sib_s, sib_r, rs_s, rs_r, st_s, st_r, ag_s, ag_r, mp_s, mp_r,
):
    hs = heads * steps
    half = hs // 2
    own = rows // nseq
    chips = nseq // 2
    me = lax.axis_index("seq")
    mp = lax.axis_index("mp")
    sec = lax.axis_index("section")
    chip, core = me // 2, me % 2
    partner = {"section": lax.rem(sec + nsec // 2, nsec)}
    sibling = {"seq": 2 * chip + 1 - core}
    away = (1, 3, 2)
    far_chip = [lax.rem(chip + k, 4) for k in away]
    far = [{"seq": 2 * c + core} for c in far_chip]
    from_chip = [lax.rem(chip + 4 - k, 4) for k in away]

    def mp_dev(k):
        return {"mp": lax.rem(mp + k, nmp)}

    def remote(src, dst, send, recv, device):
        return pltpu.make_async_remote_copy(
            src_ref=src, dst_ref=dst, send_sem=send, recv_sem=recv,
            device_id=device, device_id_type=MESH,
        )

    barrier = pltpu.get_barrier_semaphore()
    greeted = [partner, *far, *(mp_dev(k) for k in range(1, nmp)), sibling]
    for device in greeted:
        pl.semaphore_signal(barrier, inc=1, device_id=device, device_id_type=MESH)

    half_pool = slots * PAGE
    loads = [
        pltpu.make_async_copy(dq_h, dq_v, in_sem.at[0]),
        pltpu.make_async_copy(pool_h.at[0:half_pool], pool_v.at[0:half_pool], in_sem.at[1]),
        pltpu.make_async_copy(pp_h, pp_v, in_sem.at[2]),
        pltpu.make_async_copy(pool_h.at[half_pool:], pool_v.at[half_pool:], in_sem.at[3]),
        pltpu.make_async_copy(dp_h, dp_v, in_sem.at[4]),
        pltpu.make_async_copy(pq_h, pq_v, in_sem.at[5]),
        pltpu.make_async_copy(w_h, w_v, in_sem.at[6]),
    ]
    for c in loads:
        c.start()

    lane = iota((hs, 128), 1)
    lane1 = iota((8, 128), 1)
    key_lane = iota((hs, 2 * PAGE), 1)
    key_id = jnp.where(key_lane % 2 == 0, key_lane // 2, PAGE)

    def place_of(row):
        return (row % 16) // 2 * 16 + row % 2 * 8 + row // 16

    def merge(state, index, place, m, l):
        top, total, slot_top, slot_place = state
        hit = lane == place
        fresh = jnp.where(hit, jnp.maximum(top, m), top)
        total = total * jnp.exp2((top - fresh) * SCALE) + jnp.where(
            hit, l * jnp.exp2((m - fresh) * SCALE), 0.0
        )
        slot_top = jnp.where(lane == index, m, slot_top)
        slot_place = jnp.where(lane1 == index, place, slot_place)
        return fresh, total, slot_top, slot_place

    def slot_group(g, state, width):
        done = []
        for i in range(width):
            j = g * width + i
            entry = slot_s[j]
            live = entry >= 0
            row = jnp.where(live, entry // MAXP, 0)
            count = jnp.where(live, jnp.clip(ctx_s[row] - (entry % MAXP) * PAGE, 0, PAGE), 0)
            page = pool_v[pl.ds(pl.multiple_of(j * 2 * PAGE, 2 * PAGE), 2 * PAGE), :]
            place = jnp.where(live, place_of(row), -1)
            done.append((j, place, count, page, dot_nt(dq_v[row], page)))
        for j, place, count, page, scores in done:
            allowed = key_id < count
            scores = jnp.where(allowed, scores, NEG)
            m = jnp.max(scores, axis=1, keepdims=True)
            p = jnp.where(allowed, jnp.exp2((scores - m) * SCALE), 0.0)
            l = jnp.sum(p, axis=1, keepdims=True)
            acc = dot_nn(pltpu.roll(p, 1, 1).astype(BF16), page)
            accs[pl.ds(pl.multiple_of(j * hs, hs), hs), :] = acc
            state = merge(state, j, place, m, l)
        return state

    state = (
        jnp.full((hs, 128), NEG, F32), jnp.zeros((hs, 128), F32),
        jnp.full((hs, 128), NEG, F32), jnp.full((8, 128), -1, jnp.int32),
    )
    width = 4
    loads[0].wait()
    loads[1].wait()
    first = slots // width // 2
    state = lax.fori_loop(0, first, lambda g, s: slot_group(g, s, width), state)

    loads[2].wait()
    ri = iota((2 * PAGE, 2 * PAGE), 0)
    ci = iota((2 * PAGE, 2 * PAGE), 1)
    pick = jnp.where(ci == jnp.where(ri < PAGE, 2 * ri, 2 * (ri - PAGE) + 1), 1.0, 0.0).astype(BF16)
    for b in range(BLOCKS):
        both = dot_nn(pick, pp_v[b * 2 * PAGE:(b + 1) * 2 * PAGE, :]).astype(BF16)
        kv[me, b * PAGE:(b + 1) * PAGE, :] = both[:PAGE]
        kv[me, (BLOCKS + b) * PAGE:(BLOCKS + b + 1) * PAGE, :] = both[PAGE:]

    pl.semaphore_wait(barrier, len(greeted))
    q_out = remote(dq_v.at[0], q0, z_s.at[0], z_r.at[0], partner)
    q_out.start()
    kv_far = [remote(kv.at[me], kv.at[me], kv_s.at[i], kv_r.at[i], far[i]) for i in range(3)]
    for c in kv_far:
        c.start()
    kv_near = [remote(kv.at[me], kv.at[me], kv_s.at[3], kv_r.at[3], sibling)] + [
        remote(kv.at[2 * f + core], kv.at[2 * f + core], kv_s.at[4 + i], kv_r.at[4 + i], sibling)
        for i, f in enumerate(from_chip)
    ]
    kv_near[0].start()

    loads[3].wait()
    state = lax.fori_loop(first, slots // width, lambda g, s: slot_group(g, s, width), state)

    loads[4].wait()
    mine = [16 * m + 2 * me for m in range(nmp)]
    line = 2 * steps
    recent = jnp.concatenate(
        [dp_v[pl.ds(pl.multiple_of(r * line, 2 * line), 2 * line), :] for r in mine], axis=0
    )
    rq = jnp.concatenate([dq_v[pl.ds(r, 2)].reshape(2 * hs, HEAD) for r in mine], axis=0)
    scores = dot_nt(rq, recent)
    ri = iota(scores.shape, 0)
    ci = iota(scores.shape, 1)
    allowed = (
        (ci % 2 == 0) & (ci // line == ri // hs) & ((ci % line) // 2 <= ri % steps)
    )
    scores = jnp.where(allowed, scores, NEG)
    m = jnp.max(scores, axis=1, keepdims=True)
    p = jnp.where(allowed, jnp.exp2((scores - m) * SCALE), 0.0)
    l = jnp.sum(p, axis=1, keepdims=True)
    accs[slots * hs:(slots + own) * hs, :] = dot_nn(pltpu.roll(p, 1, 1).astype(BF16), recent)
    for r in range(own):
        state = merge(
            state, slots + r, me * own + r % 2 * 8 + r // 2,
            m[r * hs:(r + 1) * hs], l[r * hs:(r + 1) * hs],
        )
    top, total, slot_top, slot_place = state
    lse_mine = jnp.where(
        total > 0.0, top * SCALE + jnp.log2(jnp.maximum(total, 1e-30)), NEG
    )
    lse_out[...] = lse_mine
    lse_copy = remote(lse_out, lse_in, z_s.at[2], z_r.at[2], sibling)
    lse_copy.start()
    place_pick = jnp.where(
        iota((128, 128), 0) == jnp.broadcast_to(slot_place[0:1], (128, 128)), 1.0, 0.0
    )
    lse_copy.wait()
    peak = jnp.maximum(lse_mine, lse_in[...])
    lse_chip = peak + jnp.log2(jnp.exp2(lse_mine - peak) + jnp.exp2(lse_in[...] - peak))
    whole_slot = dot_nn(lse_chip, place_pick, lax.Precision.HIGHEST)
    factor = jnp.exp2(slot_top * SCALE - whole_slot)
    lse_t[...] = jnp.concatenate([lse_chip, jnp.zeros((128 - hs, 128), F32)], axis=0).T

    count = accs.shape[0] // hs
    sib_copies = []
    for h in range(2):
        for i in range(half):
            j = h * half + i
            weights = (place_pick * jnp.broadcast_to(factor[j:j + 1], (128, 128)))[:rows, :count]
            sums = dot_nn(
                weights.astype(BF16), accs[pl.ds(j, count, stride=hs), :].astype(BF16)
            ).astype(BF16)
            for s in range(nseq):
                part[h, s % 2, s // 2, i] = sums[s * own:(s + 1) * own]
        c = remote(part.at[h, 1 - core], sib_in.at[h], sib_s.at[h], sib_r.at[h], sibling)
        c.start()
        sib_copies.append(c)

    st_copies = [
        remote(
            lse_t.at[pl.ds(pl.multiple_of((2 * f + core) * own, own), own)], lse_t_in.at[i],
            st_s.at[i], st_r.at[i], far[i],
        )
        for i, f in enumerate(far_chip)
    ]
    for c in st_copies:
        c.start()
    rs_copies = []
    for h in range(2):
        sib_copies[h].wait()
        for f in far_chip + [chip]:
            for i in range(0, half, 4):
                sl = slice(i, i + 4)
                part[h, core, f, sl] = (
                    part[h, core, f, sl].astype(F32) + sib_in[h, f, sl].astype(F32)
                ).astype(BF16)
        for i, f in enumerate(far_chip):
            c = remote(
                part.at[h, core, f], part_in.at[h, i], rs_s.at[h, i], rs_r.at[h, i], far[i]
            )
            c.start()
            rs_copies.append(c)

    for i in range(3):
        kv_far[i].wait()
        kv_near[i + 1].start()
    for c in kv_near:
        c.wait()
    loads[5].wait()
    n = nseq * PAGE

    def prompt_keys(b):
        return kv[:, b * PAGE:(b + 1) * PAGE, :].reshape(n, HEAD)

    def prompt_values(b):
        return kv[:, (BLOCKS + b) * PAGE:(BLOCKS + b + 1) * PAGE, :].reshape(n, HEAD)

    q_out.wait()
    s0 = []
    for b in range(BLOCKS):
        scores = dot_nt(q0[...], prompt_keys(b))
        s0.append(jnp.where(iota(scores.shape, 1) + b * n < ctx_s[0], scores, NEG))
    m = functools.reduce(jnp.maximum, [jnp.max(x, axis=1, keepdims=True) for x in s0])
    p0 = [jnp.exp2((x - m) * SCALE) for x in s0]
    l = sum(jnp.sum(p, axis=1, keepdims=True) for p in p0)
    acc = sum(dot_nn(p.astype(BF16), prompt_values(b)) for b, p in enumerate(p0))
    r0_out[0:hs, :] = acc / l
    lse_prompt = jnp.broadcast_to(m * SCALE + jnp.log2(l), (hs, 128))
    r0_out[hs:hs + 8, :] = jnp.concatenate(
        [lse_prompt, jnp.zeros((128 - hs, 128), F32)], axis=0
    ).T[0:8]
    r0_copy = remote(r0_out, r0_in, z_s.at[1], z_r.at[1], partner)
    r0_copy.start()

    def prompt_piece(b, pair):
        two = pq_v[b, :, pl.ds(pl.multiple_of(pair * 2 * HEAD, 2 * HEAD), 2 * HEAD)]
        q = jnp.concatenate([two[:, :HEAD], two[:, HEAD:]], axis=0)
        s_own = dot_nt(q, prompt_keys(b))
        limit = me * PAGE + iota((2 * PAGE, n), 0) % PAGE
        s_own = jnp.where(iota((2 * PAGE, n), 1) <= limit, s_own, NEG)
        m = jnp.max(s_own, axis=1, keepdims=True)
        if b:
            s_old = dot_nt(q, prompt_keys(0))
            m = jnp.maximum(m, jnp.max(s_old, axis=1, keepdims=True))
        p = jnp.exp2((s_own - m) * SCALE)
        l = jnp.sum(p, axis=1, keepdims=True)
        o = dot_nn(p.astype(BF16), prompt_values(b))
        if b:
            p = jnp.exp2((s_old - m) * SCALE)
            l = l + jnp.sum(p, axis=1, keepdims=True)
            o = o + dot_nn(p.astype(BF16), prompt_values(0))
        o = (o / l).astype(BF16)
        pre_v[b, :, pl.ds(pl.multiple_of(pair * 2 * HEAD, 2 * HEAD), 2 * HEAD)] = jnp.concatenate(
            [o[:PAGE], o[PAGE:]], axis=1
        )

    def prompt_pieces(b, lo, hi):
        def step(i, carry):
            prompt_piece(b, i)
            return carry

        lax.fori_loop(lo, hi, step, 0)

    pairs = heads // 2
    prompt_pieces(0, 0, pairs)

    for c in st_copies:
        c.wait()
    r0_copy.wait()
    first_row = (iota((own, 128), 0) == 0) & (me == 0)
    terms = [lse_t[pl.ds(pl.multiple_of(me * own, own), own), :]] + [lse_t_in[i] for i in range(3)] + [
        jnp.where(first_row, jnp.broadcast_to(r0_in[hs:hs + 1, :], (own, 128)), NEG)
    ]
    peak = functools.reduce(jnp.maximum, terms)
    whole = peak + jnp.log2(sum(jnp.exp2(t - peak) for t in terms))
    shares = [jnp.exp2(t - whole) for t in terms]
    ag_far = []
    ag_near = []
    lines = own * steps
    for h in range(2):
        for c in rs_copies[3 * h:3 * h + 3]:
            c.wait()
        for i in range(half):
            j = h * half + i
            blocks = [part[h, core, chip, i]] + [part_in[h, k, i] for k in range(3)]
            tot = jnp.broadcast_to(r0_in[j:j + 1, :], (own, HEAD)) * shares[4][:, j:j + 1]
            for share, block in zip(shares, blocks):
                tot = tot + block.astype(F32) * share[:, j:j + 1]
            for t in range(2):
                at = j // steps * lines + t * steps + j % steps
                att_f[pl.ds(at, 8, stride=8), :] = tot[8 * t:8 * t + 8]
        sl = slice(h * half * own, (h + 1) * half * own)
        att[me, sl] = att_f[sl, :].astype(BF16)
        for i in range(3):
            c = remote(att.at[me, sl], att.at[me, sl], ag_s.at[h, i], ag_r.at[h, i], far[i])
            c.start()
            ag_far.append(c)
        c = remote(att.at[me, sl], att.at[me, sl], ag_s.at[h, 3], ag_r.at[h, 3], sibling)
        c.start()
        ag_near.append(c)

    def products(chunk, sources):
        left = jnp.concatenate(
            [
                jnp.concatenate(
                    [att[2 * f + c, h * lines:(h + 1) * lines] for h in range(heads)], axis=1
                )
                for f in sources for c in range(2)
            ],
            axis=0,
        )
        out = dot_nn(left, w_v[...])
        for m in range(nmp):
            for i in range(len(sources)):
                at = 2 * i * lines + 8 * m
                prod[m, chunk + i] = jnp.concatenate(
                    [out[at:at + 8], out[at + lines:at + lines + 8]], axis=0
                ).astype(BF16)

    mp_copies = []

    def send_products(stage, chunk, width):
        sl = pl.ds(chunk, width)
        for k in range(1, nmp):
            c = remote(
                prod.at[lax.rem(mp + k, nmp), sl], prod_in.at[k - 1, sl],
                mp_s.at[stage, k - 1], mp_r.at[stage, k - 1], mp_dev(k),
            )
            c.start()
            mp_copies.append(c)

    loads[6].wait()
    for c in ag_near:
        c.wait()
    products(0, [chip])
    send_products(0, 0, 1)
    prompt_pieces(1, 0, pairs // 2)
    forward = [
        remote(
            att.at[2 * f + core], att.at[2 * f + core], ag_s.at[2, i], ag_r.at[2, i], sibling
        )
        for i, f in enumerate(from_chip)
    ]
    for i in range(3):
        ag_far[i].wait()
        ag_far[3 + i].wait()
        forward[i].start()
    prompt_pieces(1, pairs // 2, pairs)
    pre_copy = pltpu.make_async_copy(pre_v, pre_h, out_sem)
    pre_copy.start()
    forward[0].wait()
    forward[1].wait()
    products(1, from_chip[:2])
    send_products(1, 1, 2)
    forward[2].wait()
    products(3, from_chip[2:])
    send_products(2, 3, 1)

    for stage, chunks in enumerate(((0,), (1, 2), (3,))):
        for c in mp_copies[stage * (nmp - 1):(stage + 1) * (nmp - 1)]:
            c.wait()
        for chunk in chunks:
            source = ([chip] + from_chip)[chunk]
            value = prod[mp, chunk].astype(F32)
            for k in range(nmp - 1):
                value = value + prod_in[k, chunk].astype(F32)
            for r in range(4):
                for t in range(heads):
                    mix_v[source, r * hs + t * steps:r * hs + (t + 1) * steps] = value[
                        r * steps:(r + 1) * steps, t * 128:(t + 1) * 128
                    ]
    mix_o[...] = mix_v[...].reshape(mix_o.shape).astype(BF16)
    pre_copy.wait()


def hand_over(pre_i, mix_i, pre_o, mix_o, sems):
    copies = [
        pltpu.make_async_copy(pre_i, pre_o, sems.at[0]),
        pltpu.make_async_copy(mix_i, mix_o, sems.at[1]),
    ]
    for c in copies:
        c.start()
    for c in copies:
        c.wait()


def body(
    prompt_queries, prompt_pairs, decode_queries, decode_pairs, cache_pool, out_weight,
    slot_pages, placement, context_len,
):
    nsec, nseq, nmp = (lax.axis_size(a) for a in ("section", "seq", "mp"))
    _, blocks, btok, qwidth = prompt_queries.shape
    _, rows, steps, _ = decode_queries.shape
    slots = cache_pool.shape[1]
    width = out_weight.shape[2]
    heads = qwidth // HEAD
    hs = heads * steps
    own = rows // nseq
    pq = prompt_queries[0]
    pp = prompt_pairs.reshape(blocks * btok * 2, HEAD)
    dq = decode_queries.reshape(rows, steps, heads, HEAD).transpose(0, 2, 1, 3).reshape(rows, hs, HEAD)
    dp = decode_pairs.reshape(rows * steps * 2, HEAD)
    pool = cache_pool.reshape(slots * PAGE * 2, HEAD)
    w = out_weight[0]
    count = slots + own
    any_spec = pl.BlockSpec(memory_space=pl.ANY)
    smem_spec = pl.BlockSpec(memory_space=pltpu.SMEM)
    dma = pltpu.SemaphoreType.DMA
    prefill, mixed = pl.pallas_call(
        functools.partial(kernel, nsec, nseq, nmp, slots, rows, heads, steps),
        out_shape=(
            jax.ShapeDtypeStruct(pq.shape, BF16),
            jax.ShapeDtypeStruct((own * hs, HEAD), BF16),
        ),
        in_specs=[any_spec] * 6 + [smem_spec] * 2,
        out_specs=(any_spec, pl.BlockSpec(memory_space=pltpu.VMEM)),
        scratch_shapes=[
            pltpu.VMEM(pq.shape, BF16),
            pltpu.VMEM(pp.shape, BF16),
            pltpu.VMEM(dq.shape, BF16),
            pltpu.VMEM(dp.shape, BF16),
            pltpu.VMEM(pool.shape, BF16),
            pltpu.VMEM(w.shape, BF16),
            pltpu.VMEM((nseq,) + pp.shape, BF16),
            pltpu.VMEM((hs, HEAD), BF16),
            pltpu.VMEM((hs + 8, HEAD), F32),
            pltpu.VMEM((hs + 8, HEAD), F32),
            pltpu.VMEM((hs, 128), F32),
            pltpu.VMEM((hs, 128), F32),
            pltpu.VMEM((128, 128), F32),
            pltpu.VMEM((3, own, 128), F32),
            pltpu.VMEM((count * hs, HEAD), F32),
            pltpu.VMEM((2, 2, nseq // 2, hs // 2, own, HEAD), BF16),
            pltpu.VMEM((2, nseq // 2, hs // 2, own, HEAD), BF16),
            pltpu.VMEM((2, 3, hs // 2, own, HEAD), BF16),
            pltpu.VMEM((own * hs, HEAD), F32),
            pltpu.VMEM((nseq, own * hs, HEAD), BF16),
            pltpu.VMEM((nmp, 4, 4 * steps, width), BF16),
            pltpu.VMEM((nmp - 1, 4, 4 * steps, width), BF16),
            pltpu.VMEM((4, 4 * hs, HEAD), F32),
            pltpu.VMEM(pq.shape, BF16),
            dma((7,)),
            dma,
            dma((7,)), dma((7,)),
            dma((3,)), dma((3,)),
            dma((2,)), dma((2,)),
            dma((2, 3)), dma((2, 3)),
            dma((3,)), dma((3,)),
            dma((3, 4)), dma((3, 4)),
            dma((3, nmp - 1)), dma((3, nmp - 1)),
        ],
        compiler_params=pltpu.CompilerParams(
            collective_id=0, has_side_effects=True, vmem_limit_bytes=56 * 1024 * 1024
        ),
    )(pq, pp, dq, dp, pool, w, slot_pages, context_len)
    prefill, mixed = pl.pallas_call(
        hand_over,
        out_shape=(
            jax.ShapeDtypeStruct(prefill.shape, BF16), jax.ShapeDtypeStruct(mixed.shape, BF16)
        ),
        in_specs=[any_spec] * 2,
        out_specs=(any_spec,) * 2,
        scratch_shapes=[dma((2,))],
        compiler_params=pltpu.CompilerParams(vmem_limit_bytes=56 * 1024 * 1024),
    )(prefill, mixed)
    mixed = mixed.reshape(own, width // HEAD, steps, HEAD).transpose(0, 2, 1, 3)
    mixed = mixed.reshape(own, steps, width)
    return prefill[None], mixed[None]


def solution(mesh):
    return jax.shard_map(
        body,
        mesh=mesh,
        in_specs=(
            P("section", None, "seq", "mp"),
            P("section", None, "seq", None, "mp"),
            P("section", None, None, "mp"),
            P("section", None, None, None, "mp"),
            P("section", "seq", None, None, "mp"),
            P("section", "mp", "seq"),
            P("seq"),
            P(),
            P(),
        ),
        out_specs=(P("section", None, "seq", "mp"), P("section", "mp", None, "seq")),
        check_vma=False,
    )
```

time: 74.6 us -> 70.4 us (0.944)
  local copies, waits for them, and re-layouts: 3.53 us -> 0 us
    pallas_call x1, Pallas kernels: 70.3 us -> 48.7 us  [body(): pl.pallas_call(functools.partial(kernel, nsec, nseq, nmp, slots, rows, he...]
    pallas_call x0 -> x1, Pallas kernels: none -> 21 us  [body(): pl.pallas_call(hand_over, out_shape=(jax.ShapeDtypeStruct(prefill.shape,...]
    unnamed x1 -> x0, local copies, waits for them, and re-layouts: 1.87 us -> none
    reshape x1 -> x0, local copies, waits for them, and re-layouts: 1.66 us -> none  [body(): mixed = mixed.reshape(steps, own, width).transpose(1, 0, 2)]
where the time goes in v2:
time: 70.4 us; the launch traced here: 70.3 us
  Pallas kernels  69.7 us (99%)
    pallas_call x1, Pallas kernels, body(): pl.pallas_call(functools.partial(kernel, nsec, nseq, nmp, slots, rows, he...  48.7 us
    pallas_call x1, Pallas kernels, body(): pl.pallas_call(hand_over, out_shape=(jax.ShapeDtypeStruct(prefill.shape,...  21 us

profile of v2, /device:TPU:1, one launch (start us, length us, event | category | flops | bytes accessed | tf_op | source)
XLA Modules:
  0.0 70.3 jit_solution(10223075017399516970)
XLA Ops:
  0.6 48.7 %shard_map.95 = (bf16[2,128,1024]{2,1,0:T(8,128)(2,1)}, bf16[512,128]{1,0:T(8,128)(2,1)}) custom-call(bf16[2,128,1024]{2,1,0:T(8,128)(2,1)} %bitcast.19, bf16[512,128]{1,0:T(8,128)(2,1)} %bitcast.21, bf16[128,32,128]{2,1,0:T(8,128)(2,1)} %bitcast.18, bf16[1024,128]{1,0:T(8,128)(2,1)} %bitcast.20, bf16[12288,128]{1,0:T(8,128)(2,1)} %bitcast.16, ...), custom_call_target="tpu_custom_call" | custom-call | tf_op jit(solution)/shard_map/pallas_call | solution.py:446
  49.3 21.0 %shard_map.96 = (bf16[2,128,1024]{2,1,0:T(8,128)(2,1)}, bf16[512,128]{1,0:T(8,128)(2,1)}) custom-call(bf16[2,128,1024]{2,1,0:T(8,128)(2,1)} %get-tuple-element.6.pre_i, bf16[512,128]{1,0:T(8,128)(2,1)} %get-tuple-element.7.mix_i), custom_call_target="tpu_custom_call" | custom-call | tf_op jit(solution)/shard_map/pallas_call | solution.py:493

commit v3 on v2

--- a/solution.py
+++ b/solution.py
@@ -38,8 +38,8 @@
     pq_h, pp_h, dq_h, dp_h, pool_h, w_h, slot_s, ctx_s,
     pre_h, mix_o,
     pq_v, pp_v, dq_v, dp_v, pool_v, w_v, kv, q0, r0_out, r0_in, lse_out, lse_in, lse_t, lse_t_in,
-    accs, part, sib_in, part_in, att_f, att, prod, prod_in, mix_v, pre_v,
-    in_sem, out_sem, kv_s, kv_r, z_s, z_r, sib_s, sib_r, rs_s, rs_r, st_s, st_r, ag_s, ag_r, mp_s, mp_r,
+    accs, part, sib_in, part_in, att, prod_f, prod, prod_in, mix_v, pre_v,
+    in_sem, out_sem, kv_s, kv_r, z_s, z_r, sib_s, sib_r, rs_s, rs_r, st_s, st_r, ag_s, ag_r, fw_s, fw_r, mp_s, mp_r,
 ):
     hs = heads * steps
     half = hs // 2
@@ -70,7 +70,7 @@
     for device in greeted:
         pl.semaphore_signal(barrier, inc=1, device_id=device, device_id_type=MESH)
 
-    half_pool = slots * PAGE
+    half_pool = slots * PAGE * 4 // 3
     loads = [
         pltpu.make_async_copy(dq_h, dq_v, in_sem.at[0]),
         pltpu.make_async_copy(pool_h.at[0:half_pool], pool_v.at[0:half_pool], in_sem.at[1]),
@@ -131,7 +131,7 @@
     width = 4
     loads[0].wait()
     loads[1].wait()
-    first = slots // width // 2
+    first = slots // width * 2 // 3
     state = lax.fori_loop(0, first, lambda g, s: slot_group(g, s, width), state)
 
     loads[2].wait()
@@ -199,19 +199,24 @@
     lse_t[...] = jnp.concatenate([lse_chip, jnp.zeros((128 - hs, 128), F32)], axis=0).T
 
     count = accs.shape[0] // hs
-    sib_copies = []
-    for h in range(2):
-        for i in range(half):
-            j = h * half + i
-            weights = (place_pick * jnp.broadcast_to(factor[j:j + 1], (128, 128)))[:rows, :count]
-            sums = dot_nn(
-                weights.astype(BF16), accs[pl.ds(j, count, stride=hs), :].astype(BF16)
-            ).astype(BF16)
-            for s in range(nseq):
-                part[h, s % 2, s // 2, i] = sums[s * own:(s + 1) * own]
-        c = remote(part.at[h, 1 - core], sib_in.at[h], sib_s.at[h], sib_r.at[h], sibling)
-        c.start()
-        sib_copies.append(c)
+
+    def row_sums(j):
+        weights = (place_pick * jnp.broadcast_to(factor[j:j + 1], (128, 128)))[:rows, :count]
+        return dot_nn(weights.astype(BF16), accs[pl.ds(j, count, stride=hs), :].astype(BF16))
+
+    for i in range(half):
+        even, odd = row_sums(2 * i), row_sums(2 * i + 1)
+        for s in range(nseq):
+            for t in range(2):
+                sl = slice(s * own + 8 * t, s * own + 8 * t + 8)
+                part[t, s % 2, s // 2, i] = jnp.concatenate([even[sl], odd[sl]], axis=0).astype(BF16)
+    order = (1, 0)
+    sib_copies = [
+        remote(part.at[t, 1 - core], sib_in.at[t], sib_s.at[t], sib_r.at[t], sibling)
+        for t in range(2)
+    ]
+    for t in order:
+        sib_copies[t].start()
 
     st_copies = [
         remote(
@@ -220,23 +225,26 @@
         )
         for i, f in enumerate(far_chip)
     ]
-    for c in st_copies:
-        c.start()
-    rs_copies = []
-    for h in range(2):
-        sib_copies[h].wait()
-        for f in far_chip + [chip]:
-            for i in range(0, half, 4):
-                sl = slice(i, i + 4)
-                part[h, core, f, sl] = (
-                    part[h, core, f, sl].astype(F32) + sib_in[h, f, sl].astype(F32)
+    rs_copies = [
+        [
+            remote(part.at[t, core, f], part_in.at[t, i], rs_s.at[t, i], rs_r.at[t, i], far[i])
+            for i, f in enumerate(far_chip)
+        ]
+        for t in range(2)
+    ]
+    for t in order:
+        sib_copies[t].wait()
+        for i, f in enumerate(far_chip + [chip]):
+            for at in range(0, half, 4):
+                sl = slice(at, at + 4)
+                part[t, core, f, sl] = (
+                    part[t, core, f, sl].astype(F32) + sib_in[t, f, sl].astype(F32)
                 ).astype(BF16)
-        for i, f in enumerate(far_chip):
-            c = remote(
-                part.at[h, core, f], part_in.at[h, i], rs_s.at[h, i], rs_r.at[h, i], far[i]
-            )
-            c.start()
-            rs_copies.append(c)
+            if i < 3:
+                rs_copies[t][i].start()
+        if t == order[0]:
+            for c in st_copies:
+                c.start()
 
     for i in range(3):
         kv_far[i].wait()
@@ -299,65 +307,88 @@
         lax.fori_loop(lo, hi, step, 0)
 
     pairs = heads // 2
-    prompt_pieces(0, 0, pairs)
+    prompt_pieces(0, 0, pairs // 2)
 
     for c in st_copies:
         c.wait()
-    r0_copy.wait()
-    first_row = (iota((own, 128), 0) == 0) & (me == 0)
-    terms = [lse_t[pl.ds(pl.multiple_of(me * own, own), own), :]] + [lse_t_in[i] for i in range(3)] + [
-        jnp.where(first_row, jnp.broadcast_to(r0_in[hs:hs + 1, :], (own, 128)), NEG)
-    ]
-    peak = functools.reduce(jnp.maximum, terms)
-    whole = peak + jnp.log2(sum(jnp.exp2(t - peak) for t in terms))
-    shares = [jnp.exp2(t - whole) for t in terms]
     ag_far = []
     ag_near = []
-    lines = own * steps
-    for h in range(2):
-        for c in rs_copies[3 * h:3 * h + 3]:
+    lines = 8 * steps
+
+    def shares_of(terms):
+        peak = functools.reduce(jnp.maximum, terms)
+        whole = peak + jnp.log2(sum(jnp.exp2(t - peak) for t in terms))
+        return [jnp.exp2(t - whole) for t in terms]
+
+    def finish(t):
+        sl = slice(8 * t, 8 * t + 8)
+        mine_t = lse_t[pl.ds(pl.multiple_of(me * own + 8 * t, 8), 8), :]
+        terms = [mine_t] + [lse_t_in[i, sl] for i in range(3)]
+        if t == 0:
+            r0_copy.wait()
+            first_row = (iota((8, 128), 0) == 0) & (me == 0)
+            terms.append(jnp.where(first_row, jnp.broadcast_to(r0_in[hs:hs + 1, :], (8, 128)), NEG))
+        shares = shares_of(terms)
+        for c in rs_copies[t]:
             c.wait()
         for i in range(half):
-            j = h * half + i
-            blocks = [part[h, core, chip, i]] + [part_in[h, k, i] for k in range(3)]
-            tot = jnp.broadcast_to(r0_in[j:j + 1, :], (own, HEAD)) * shares[4][:, j:j + 1]
-            for share, block in zip(shares, blocks):
-                tot = tot + block.astype(F32) * share[:, j:j + 1]
-            for t in range(2):
-                at = j // steps * lines + t * steps + j % steps
-                att_f[pl.ds(at, 8, stride=8), :] = tot[8 * t:8 * t + 8]
-        sl = slice(h * half * own, (h + 1) * half * own)
-        att[me, sl] = att_f[sl, :].astype(BF16)
-        for i in range(3):
-            c = remote(att.at[me, sl], att.at[me, sl], ag_s.at[h, i], ag_r.at[h, i], far[i])
-            c.start()
-            ag_far.append(c)
-        c = remote(att.at[me, sl], att.at[me, sl], ag_s.at[h, 3], ag_r.at[h, 3], sibling)
+            blocks = [part[t, core, chip, i]] + [part_in[t, k, i] for k in range(3)]
+            blocks = [b.astype(F32) for b in blocks]
+            two = []
+            for j in range(2):
+                at = 2 * i + j
+                tot = sum(
+                    b[8 * j:8 * j + 8] * share[:, at:at + 1] for b, share in zip(blocks, shares)
+                )
+                if t == 0:
+                    tot = tot + jnp.broadcast_to(r0_in[at:at + 1, :], (8, HEAD)) * shares[4][:, at:at + 1]
+                two.append(tot)
+            att[t, me, 16 * i:16 * i + 16] = jnp.concatenate(two, axis=0).astype(BF16)
+        block = att.at[t, me]
+        c = remote(block, block, ag_s.at[t, 3], ag_r.at[t, 3], sibling)
         c.start()
         ag_near.append(c)
-
-    def products(chunk, sources):
+        group = [remote(block, block, ag_s.at[t, i], ag_r.at[t, i], far[i]) for i in range(3)]
+        for c in group:
+            c.start()
+        ag_far.append(group)
+
+    finish(order[0])
+    prompt_pieces(0, pairs // 2, pairs)
+    finish(order[1])
+
+    half_cols = w_v.shape[1] // 2
+
+    def products(first_unit, sources):
         left = jnp.concatenate(
             [
                 jnp.concatenate(
-                    [att[2 * f + c, h * lines:(h + 1) * lines] for h in range(heads)], axis=1
+                    [att[t, 2 * f + c, h * lines:(h + 1) * lines] for h in range(heads)], axis=1
                 )
-                for f in sources for c in range(2)
+                for t, f in sources for c in range(2)
             ],
             axis=0,
         )
         out = dot_nn(left, w_v[...])
-        for m in range(nmp):
-            for i in range(len(sources)):
-                at = 2 * i * lines + 8 * m
-                prod[m, chunk + i] = jnp.concatenate(
-                    [out[at:at + 8], out[at + lines:at + lines + 8]], axis=0
+        for k in range(heads):
+            prod_f[k, 0:2 * lines * len(sources), :] = out[:, 128 * k:128 * (k + 1)]
+        for i in range(len(sources)):
+            for m in range(nmp):
+                value = jnp.concatenate(
+                    [
+                        prod_f[k, pl.ds(2 * lines * i + m, 8, stride=8), :]
+                        for k in range(heads)
+                    ],
+                    axis=1,
+                )
+                prod[m, first_unit + i] = jnp.concatenate(
+                    [value[:, :half_cols], value[:, half_cols:]], axis=0
                 ).astype(BF16)
 
     mp_copies = []
 
-    def send_products(stage, chunk, width):
-        sl = pl.ds(chunk, width)
+    def send_products(stage, first_unit, units):
+        sl = pl.ds(first_unit, units)
         for k in range(1, nmp):
             c = remote(
                 prod.at[lax.rem(mp + k, nmp), sl], prod_in.at[k - 1, sl],
@@ -369,43 +400,39 @@
     loads[6].wait()
     for c in ag_near:
         c.wait()
-    products(0, [chip])
-    send_products(0, 0, 1)
-    prompt_pieces(1, 0, pairs // 2)
-    forward = [
-        remote(
-            att.at[2 * f + core], att.at[2 * f + core], ag_s.at[2, i], ag_r.at[2, i], sibling
-        )
-        for i, f in enumerate(from_chip)
-    ]
-    for i in range(3):
-        ag_far[i].wait()
-        ag_far[3 + i].wait()
-        forward[i].start()
-    prompt_pieces(1, pairs // 2, pairs)
+    products(0, [(t, chip) for t in order])
+    send_products(0, 0, 2)
+    for turn, t in enumerate(order):
+        forward = []
+        for i, f in enumerate(from_chip):
+            ag_far[turn][i].wait()
+            block = att.at[t, 2 * f + core]
+            c = remote(block, block, fw_s.at[t, i], fw_r.at[t, i], sibling)
+            c.start()
+            forward.append(c)
+        for c in forward:
+            c.wait()
+        products(2 + 3 * turn, [(t, f) for f in from_chip])
+        send_products(1 + turn, 2 + 3 * turn, 3)
+        prompt_pieces(1, turn * pairs // 2, (turn + 1) * pairs // 2)
     pre_copy = pltpu.make_async_copy(pre_v, pre_h, out_sem)
     pre_copy.start()
-    forward[0].wait()
-    forward[1].wait()
-    products(1, from_chip[:2])
-    send_products(1, 1, 2)
-    forward[2].wait()
-    products(3, from_chip[2:])
-    send_products(2, 3, 1)
-
-    for stage, chunks in enumerate(((0,), (1, 2), (3,))):
+
+    units = [(t, chip) for t in order] + [(t, f) for t in order for f in from_chip]
+    for stage, (lo, hi) in enumerate(((0, 2), (2, 5), (5, 8))):
         for c in mp_copies[stage * (nmp - 1):(stage + 1) * (nmp - 1)]:
             c.wait()
-        for chunk in chunks:
-            source = ([chip] + from_chip)[chunk]
-            value = prod[mp, chunk].astype(F32)
+        for unit in range(lo, hi):
+            t, source = units[unit]
+            value = prod[mp, unit].astype(F32)
             for k in range(nmp - 1):
-                value = value + prod_in[k, chunk].astype(F32)
-            for r in range(4):
-                for t in range(heads):
-                    mix_v[source, r * hs + t * steps:r * hs + (t + 1) * steps] = value[
-                        r * steps:(r + 1) * steps, t * 128:(t + 1) * 128
-                    ]
+                value = value + prod_in[k, unit].astype(F32)
+            for c in range(2):
+                for k in range(heads):
+                    at = (2 * c + t) * hs + k * steps
+                    row = k // (heads // 2) * 8 + c * steps
+                    col = k % (heads // 2) * 128
+                    mix_v[source, at:at + steps] = value[row:row + steps, col:col + 128]
     mix_o[...] = mix_v[...].reshape(mix_o.shape).astype(BF16)
     pre_copy.wait()
 
@@ -470,10 +497,10 @@
             pltpu.VMEM((2, 2, nseq // 2, hs // 2, own, HEAD), BF16),
             pltpu.VMEM((2, nseq // 2, hs // 2, own, HEAD), BF16),
             pltpu.VMEM((2, 3, hs // 2, own, HEAD), BF16),
-            pltpu.VMEM((own * hs, HEAD), F32),
-            pltpu.VMEM((nseq, own * hs, HEAD), BF16),
-            pltpu.VMEM((nmp, 4, 4 * steps, width), BF16),
-            pltpu.VMEM((nmp - 1, 4, 4 * steps, width), BF16),
+            pltpu.VMEM((2, nseq, own * hs // 2, HEAD), BF16),
+            pltpu.VMEM((width // 128, 48 * steps, 128), F32),
+            pltpu.VMEM((nmp, 8, 16, width // 2), BF16),
+            pltpu.VMEM((nmp - 1, 8, 16, width // 2), BF16),
             pltpu.VMEM((4, 4 * hs, HEAD), F32),
             pltpu.VMEM(pq.shape, BF16),
             dma((7,)),
@@ -483,7 +510,8 @@
             dma((2,)), dma((2,)),
             dma((2, 3)), dma((2, 3)),
             dma((3,)), dma((3,)),
-            dma((3, 4)), dma((3, 4)),
+            dma((2, 4)), dma((2, 4)),
+            dma((2, 3)), dma((2, 3)),
             dma((3, nmp - 1)), dma((3, nmp - 1)),
         ],
         compiler_params=pltpu.CompilerParams(
@@ -495,10 +523,9 @@
         out_shape=(
             jax.ShapeDtypeStruct(prefill.shape, BF16), jax.ShapeDtypeStruct(mixed.shape, BF16)
         ),
-        in_specs=[any_spec] * 2,
+        in_specs=[pl.BlockSpec(memory_space=pltpu.VMEM)] * 2,
         out_specs=(any_spec,) * 2,
         scratch_shapes=[dma((2,))],
-        compiler_params=pltpu.CompilerParams(vmem_limit_bytes=56 * 1024 * 1024),
     )(prefill, mixed)
     mixed = mixed.reshape(own, width // HEAD, steps, HEAD).transpose(0, 2, 1, 3)
     mixed = mixed.reshape(own, steps, width)

time: 70.4 us -> 49.1 us (0.70)
  Pallas kernels: 69.7 us -> 48.4 us
    pallas_call x1, Pallas kernels: 21 us -> 1.91 us  [body(): pl.pallas_call(hand_over, out_shape=(jax.ShapeDtypeStruct(prefill.shape,...]
    pallas_call x1, Pallas kernels: 48.7 us -> 46.5 us  [body(): pl.pallas_call(functools.partial(kernel, nsec, nseq, nmp, slots, rows, he...]
where the time goes in v3:
time: 49.1 us; the launch traced here: 49 us
  Pallas kernels  48.4 us (99%)
  between operations  0.64 us (1%)
    pallas_call x1, Pallas kernels, body(): pl.pallas_call(functools.partial(kernel, nsec, nseq, nmp, slots, rows, he...  46.5 us
    pallas_call x1, Pallas kernels, body(): pl.pallas_call(hand_over, out_shape=(jax.ShapeDtypeStruct(prefill.shape,...  1.91 us

profile of v3, /device:TPU:1, one launch (start us, length us, event | category | flops | bytes accessed | tf_op | source)
XLA Modules:
  0.0 49.0 jit_solution(9564963031543995858)
XLA Ops:
  0.6 46.5 %shard_map.95 = (bf16[2,128,1024]{2,1,0:T(8,128)(2,1)}, bf16[512,128]{1,0:T(8,128)(2,1)}) custom-call(bf16[2,128,1024]{2,1,0:T(8,128)(2,1)} %bitcast.19, bf16[512,128]{1,0:T(8,128)(2,1)} %bitcast.21, bf16[128,32,128]{2,1,0:T(8,128)(2,1)} %bitcast.18, bf16[1024,128]{1,0:T(8,128)(2,1)} %bitcast.20, bf16[12288,128]{1,0:T(8,128)(2,1)} %bitcast.16, ...), custom_call_target="tpu_custom_call" | custom-call | tf_op jit(solution)/shard_map/pallas_call | solution.py:473
  47.1 1.9 %shard_map.96 = (bf16[2,128,1024]{2,1,0:T(8,128)(2,1)}, bf16[512,128]{1,0:T(8,128)(2,1)}) custom-call(bf16[2,128,1024]{2,1,0:T(8,128)(2,1)} %get-tuple-element.6.pre_i, bf16[512,128]{1,0:T(8,128)(2,1)} %get-tuple-element.7.mix_i), custom_call_target="tpu_custom_call" | custom-call | tf_op jit(solution)/shard_map/pallas_call | solution.py:521

commit v4 on v3

--- a/solution.py
+++ b/solution.py
@@ -37,9 +37,10 @@
     nsec, nseq, nmp, slots, rows, heads, steps,
     pq_h, pp_h, dq_h, dp_h, pool_h, w_h, slot_s, ctx_s,
     pre_h, mix_o,
-    pq_v, pp_v, dq_v, dp_v, pool_v, w_v, kv, q0, r0_out, r0_in, lse_out, lse_in, lse_t, lse_t_in,
+    pq_v, pp_v, dq_v, dp_v, pool_v, w_v, kv, q0, r0_out, r0_in, r0_mix, r0_mix_in,
+    lse_out, lse_in, lse_t, lse_t_in,
     accs, part, sib_in, part_in, att, prod_f, prod, prod_in, mix_v, pre_v,
-    in_sem, out_sem, kv_s, kv_r, z_s, z_r, sib_s, sib_r, rs_s, rs_r, st_s, st_r, ag_s, ag_r, fw_s, fw_r, mp_s, mp_r,
+    in_sem, out_sem, kv_s, kv_r, z_s, z_r, r0_s, r0_r, sib_s, sib_r, rs_s, rs_r, st_s, st_r, ag_s, ag_r, fw_s, fw_r, mp_s, mp_r,
 ):
     hs = heads * steps
     half = hs // 2
@@ -49,7 +50,8 @@
     mp = lax.axis_index("mp")
     sec = lax.axis_index("section")
     chip, core = me // 2, me % 2
-    partner = {"section": lax.rem(sec + nsec // 2, nsec)}
+    next_sec = {"section": lax.rem(sec + 1, nsec)}
+    last_sec = {"section": lax.rem(sec + nsec - 1, nsec)}
     sibling = {"seq": 2 * chip + 1 - core}
     away = (1, 3, 2)
     far_chip = [lax.rem(chip + k, 4) for k in away]
@@ -66,21 +68,25 @@
         )
 
     barrier = pltpu.get_barrier_semaphore()
-    greeted = [partner, *far, *(mp_dev(k) for k in range(1, nmp)), sibling]
+    greeted = [*(mp_dev(k) for k in range(1, nmp)), next_sec, last_sec, *far, sibling]
     for device in greeted:
         pl.semaphore_signal(barrier, inc=1, device_id=device, device_id_type=MESH)
 
-    half_pool = slots * PAGE * 4 // 3
-    loads = [
-        pltpu.make_async_copy(dq_h, dq_v, in_sem.at[0]),
-        pltpu.make_async_copy(pool_h.at[0:half_pool], pool_v.at[0:half_pool], in_sem.at[1]),
-        pltpu.make_async_copy(pp_h, pp_v, in_sem.at[2]),
-        pltpu.make_async_copy(pool_h.at[half_pool:], pool_v.at[half_pool:], in_sem.at[3]),
-        pltpu.make_async_copy(dp_h, dp_v, in_sem.at[4]),
-        pltpu.make_async_copy(pq_h, pq_v, in_sem.at[5]),
-        pltpu.make_async_copy(w_h, w_v, in_sem.at[6]),
-    ]
-    for c in loads:
+    width = 12
+    groups = slots // width
+    group_lines = width * 2 * PAGE
+
+    def pool_load(g):
+        sl = slice(g * group_lines, (g + 1) * group_lines)
+        return pltpu.make_async_copy(pool_h.at[sl], pool_v.at[sl], in_sem.at[5 + g])
+
+    load_dq = pltpu.make_async_copy(dq_h, dq_v, in_sem.at[0])
+    load_dp = pltpu.make_async_copy(dp_h, dp_v, in_sem.at[1])
+    load_pp = pltpu.make_async_copy(pp_h, pp_v, in_sem.at[2])
+    load_pq = pltpu.make_async_copy(pq_h, pq_v, in_sem.at[3])
+    load_w = pltpu.make_async_copy(w_h, w_v, in_sem.at[4])
+    load_pool = [pool_load(g) for g in range(groups)]
+    for c in [load_dq, *load_pool, load_dp, load_pp, load_pq, load_w]:
         c.start()
 
     lane = iota((hs, 128), 1)
@@ -128,13 +134,12 @@
         jnp.full((hs, 128), NEG, F32), jnp.zeros((hs, 128), F32),
         jnp.full((hs, 128), NEG, F32), jnp.full((8, 128), -1, jnp.int32),
     )
-    width = 4
-    loads[0].wait()
-    loads[1].wait()
-    first = slots // width * 2 // 3
-    state = lax.fori_loop(0, first, lambda g, s: slot_group(g, s, width), state)
-
-    loads[2].wait()
+    load_dq.wait()
+    for g in range(groups):
+        load_pool[g].wait()
+        state = slot_group(g, state, width)
+
+    load_pp.wait()
     ri = iota((2 * PAGE, 2 * PAGE), 0)
     ci = iota((2 * PAGE, 2 * PAGE), 1)
     pick = jnp.where(ci == jnp.where(ri < PAGE, 2 * ri, 2 * (ri - PAGE) + 1), 1.0, 0.0).astype(BF16)
@@ -143,22 +148,7 @@
         kv[me, b * PAGE:(b + 1) * PAGE, :] = both[:PAGE]
         kv[me, (BLOCKS + b) * PAGE:(BLOCKS + b + 1) * PAGE, :] = both[PAGE:]
 
-    pl.semaphore_wait(barrier, len(greeted))
-    q_out = remote(dq_v.at[0], q0, z_s.at[0], z_r.at[0], partner)
-    q_out.start()
-    kv_far = [remote(kv.at[me], kv.at[me], kv_s.at[i], kv_r.at[i], far[i]) for i in range(3)]
-    for c in kv_far:
-        c.start()
-    kv_near = [remote(kv.at[me], kv.at[me], kv_s.at[3], kv_r.at[3], sibling)] + [
-        remote(kv.at[2 * f + core], kv.at[2 * f + core], kv_s.at[4 + i], kv_r.at[4 + i], sibling)
-        for i, f in enumerate(from_chip)
-    ]
-    kv_near[0].start()
-
-    loads[3].wait()
-    state = lax.fori_loop(first, slots // width, lambda g, s: slot_group(g, s, width), state)
-
-    loads[4].wait()
+    load_dp.wait()
     mine = [16 * m + 2 * me for m in range(nmp)]
     line = 2 * steps
     recent = jnp.concatenate(
@@ -186,8 +176,30 @@
         total > 0.0, top * SCALE + jnp.log2(jnp.maximum(total, 1e-30)), NEG
     )
     lse_out[...] = lse_mine
-    lse_copy = remote(lse_out, lse_in, z_s.at[2], z_r.at[2], sibling)
+    scores = dot_nt(dq_v[0], dp_v[0:2 * line, :])
+    ci = iota(scores.shape, 1)
+    allowed = (ci % 2 == 0) & (ci < line) & (ci // 2 <= iota(scores.shape, 0) % steps)
+    scores = jnp.where(allowed, scores, NEG)
+    row0_m = jnp.max(scores, axis=1, keepdims=True)
+    p = jnp.where(allowed, jnp.exp2((scores - row0_m) * SCALE), 0.0)
+    row0_l = jnp.sum(p, axis=1, keepdims=True)
+    p = jnp.concatenate([jnp.zeros((hs, 1), F32), p[:, :2 * line - 1]], axis=1)
+    row0_acc = dot_nn(p.astype(BF16), dp_v[0:2 * line, :])
+
+    pl.semaphore_wait(barrier, len(greeted))
+    lse_copy = remote(lse_out, lse_in, z_s.at[0], z_r.at[0], sibling)
     lse_copy.start()
+    q_first = remote(dq_v.at[0], q0.at[0], z_s.at[1], z_r.at[1], next_sec)
+    q_second = remote(q0.at[0], q0.at[1], z_s.at[2], z_r.at[2], next_sec)
+    q_first.start()
+    kv_far = [remote(kv.at[me], kv.at[me], kv_s.at[i], kv_r.at[i], far[i]) for i in range(3)]
+    for c in kv_far:
+        c.start()
+    kv_near = [remote(kv.at[me], kv.at[me], kv_s.at[3], kv_r.at[3], sibling)] + [
+        remote(kv.at[2 * f + core], kv.at[2 * f + core], kv_s.at[4 + i], kv_r.at[4 + i], sibling)
+        for i, f in enumerate(from_chip)
+    ]
+    kv_near[0].start()
     place_pick = jnp.where(
         iota((128, 128), 0) == jnp.broadcast_to(slot_place[0:1], (128, 128)), 1.0, 0.0
     )
@@ -246,12 +258,15 @@
             for c in st_copies:
                 c.start()
 
+    q_first.wait()
+    q_second.start()
+
     for i in range(3):
         kv_far[i].wait()
         kv_near[i + 1].start()
     for c in kv_near:
         c.wait()
-    loads[5].wait()
+    load_pq.wait()
     n = nseq * PAGE
 
     def prompt_keys(b):
@@ -260,22 +275,19 @@
     def prompt_values(b):
         return kv[:, (BLOCKS + b) * PAGE:(BLOCKS + b + 1) * PAGE, :].reshape(n, HEAD)
 
-    q_out.wait()
+    q_second.wait()
     s0 = []
     for b in range(BLOCKS):
-        scores = dot_nt(q0[...], prompt_keys(b))
+        scores = dot_nt(q0[1], prompt_keys(b))
         s0.append(jnp.where(iota(scores.shape, 1) + b * n < ctx_s[0], scores, NEG))
     m = functools.reduce(jnp.maximum, [jnp.max(x, axis=1, keepdims=True) for x in s0])
     p0 = [jnp.exp2((x - m) * SCALE) for x in s0]
     l = sum(jnp.sum(p, axis=1, keepdims=True) for p in p0)
-    acc = sum(dot_nn(p.astype(BF16), prompt_values(b)) for b, p in enumerate(p0))
-    r0_out[0:hs, :] = acc / l
-    lse_prompt = jnp.broadcast_to(m * SCALE + jnp.log2(l), (hs, 128))
-    r0_out[hs:hs + 8, :] = jnp.concatenate(
-        [lse_prompt, jnp.zeros((128 - hs, 128), F32)], axis=0
-    ).T[0:8]
-    r0_copy = remote(r0_out, r0_in, z_s.at[1], z_r.at[1], partner)
-    r0_copy.start()
+    r0_out[0:hs, :] = sum(dot_nn(p.astype(BF16), prompt_values(b)) for b, p in enumerate(p0))
+    r0_out[hs:2 * hs, :] = jnp.where(lane == 0, m, l)
+    r0_first = remote(r0_out, r0_in.at[0], z_s.at[3], z_r.at[3], next_sec)
+    r0_second = remote(r0_in.at[0], r0_in.at[1], z_s.at[4], z_r.at[4], next_sec)
+    r0_first.start()
 
     def prompt_piece(b, pair):
         two = pq_v[b, :, pl.ds(pl.multiple_of(pair * 2 * HEAD, 2 * HEAD), 2 * HEAD)]
@@ -307,7 +319,7 @@
         lax.fori_loop(lo, hi, step, 0)
 
     pairs = heads // 2
-    prompt_pieces(0, 0, pairs // 2)
+    prompt_pieces(0, 0, 1)
 
     for c in st_copies:
         c.wait()
@@ -324,10 +336,6 @@
         sl = slice(8 * t, 8 * t + 8)
         mine_t = lse_t[pl.ds(pl.multiple_of(me * own + 8 * t, 8), 8), :]
         terms = [mine_t] + [lse_t_in[i, sl] for i in range(3)]
-        if t == 0:
-            r0_copy.wait()
-            first_row = (iota((8, 128), 0) == 0) & (me == 0)
-            terms.append(jnp.where(first_row, jnp.broadcast_to(r0_in[hs:hs + 1, :], (8, 128)), NEG))
         shares = shares_of(terms)
         for c in rs_copies[t]:
             c.wait()
@@ -340,8 +348,6 @@
                 tot = sum(
                     b[8 * j:8 * j + 8] * share[:, at:at + 1] for b, share in zip(blocks, shares)
                 )
-                if t == 0:
-                    tot = tot + jnp.broadcast_to(r0_in[at:at + 1, :], (8, HEAD)) * shares[4][:, at:at + 1]
                 two.append(tot)
             att[t, me, 16 * i:16 * i + 16] = jnp.concatenate(two, axis=0).astype(BF16)
         block = att.at[t, me]
@@ -352,10 +358,6 @@
         for c in group:
             c.start()
         ag_far.append(group)
-
-    finish(order[0])
-    prompt_pieces(0, pairs // 2, pairs)
-    finish(order[1])
 
     half_cols = w_v.shape[1] // 2
 
@@ -397,29 +399,82 @@
             c.start()
             mp_copies.append(c)
 
-    loads[6].wait()
-    for c in ag_near:
-        c.wait()
-    products(0, [(t, chip) for t in order])
-    send_products(0, 0, 2)
-    for turn, t in enumerate(order):
-        forward = []
+    def forward_rows(turn):
+        copies = []
         for i, f in enumerate(from_chip):
             ag_far[turn][i].wait()
-            block = att.at[t, 2 * f + core]
-            c = remote(block, block, fw_s.at[t, i], fw_r.at[t, i], sibling)
+            block = att.at[order[turn], 2 * f + core]
+            c = remote(block, block, fw_s.at[turn, i], fw_r.at[turn, i], sibling)
             c.start()
-            forward.append(c)
-        for c in forward:
-            c.wait()
-        products(2 + 3 * turn, [(t, f) for f in from_chip])
-        send_products(1 + turn, 2 + 3 * turn, 3)
-        prompt_pieces(1, turn * pairs // 2, (turn + 1) * pairs // 2)
+            copies.append(c)
+        return copies
+
+    finish(order[0])
+    load_w.wait()
+    ag_near[0].wait()
+    products(0, [(order[0], chip)])
+    send_products(0, 0, 1)
+    r0_first.wait()
+    r0_second.start()
+    finish(order[1])
+    prompt_pieces(0, 1, 2)
+    ag_near[1].wait()
+    products(1, [(order[1], chip)])
+    send_products(1, 1, 1)
+    prompt_pieces(0, 2, 3)
+    forward = forward_rows(0)
+    prompt_pieces(0, 3, pairs)
+    for c in forward:
+        c.wait()
+    products(2, [(order[0], f) for f in from_chip])
+    send_products(2, 2, 3)
+    forward = forward_rows(1)
+
+    r0_second.wait()
+    prompt_m, prompt_l = r0_in[1, hs:2 * hs, 0:1], r0_in[1, hs:2 * hs, 1:2]
+    peak = jnp.maximum(row0_m, prompt_m)
+    keep = jnp.exp2((row0_m - peak) * SCALE)
+    more = jnp.exp2((prompt_m - peak) * SCALE)
+    row0 = (row0_acc * keep + r0_in[1, 0:hs, :] * more) / (row0_l * keep + prompt_l * more)
+    row0 = jnp.concatenate([row0[h * steps:(h + 1) * steps] for h in range(heads)], axis=1)
+    row0 = jnp.concatenate([row0, jnp.zeros((16 - steps, row0.shape[1]), F32)], axis=0)
+    row0 = dot_nn(row0.astype(BF16), w_v[...])[0:8]
+    row0 = jnp.concatenate([row0[:, :half_cols], row0[:, half_cols:]], axis=0)
+    r0_mix[...] = row0.astype(BF16)
+
+    def row0_copy(k):
+        return remote(r0_mix, r0_mix_in.at[k - 1], r0_s.at[k - 1], r0_r.at[k - 1], {"mp": 0})
+
+    for k in range(1, nmp):
+        @pl.when(mp == k)
+        def _(k=k):
+            row0_copy(k).start()
+
+    for c in forward:
+        c.wait()
+    products(5, [(order[1], f) for f in from_chip])
+    send_products(3, 5, 3)
+    prompt_pieces(1, 0, pairs)
     pre_copy = pltpu.make_async_copy(pre_v, pre_h, out_sem)
     pre_copy.start()
 
-    units = [(t, chip) for t in order] + [(t, f) for t in order for f in from_chip]
-    for stage, (lo, hi) in enumerate(((0, 2), (2, 5), (5, 8))):
+    for k in range(1, nmp):
+        @pl.when(mp == k)
+        def _(k=k):
+            row0_copy(k).wait_send()
+            r0_mix_in[...] = jnp.zeros(r0_mix_in.shape, BF16)
+
+    @pl.when(mp == 0)
+    def _():
+        for k in range(1, nmp):
+            row0_copy(k).wait_recv()
+
+    for k in range(nmp - 1):
+        row0 = row0 + r0_mix_in[k].astype(F32)
+
+    units = [(t, chip) for t in order]
+    units = units + [(t, f) for t in order for f in from_chip]
+    for stage, (lo, hi) in enumerate(((0, 1), (1, 2), (2, 5), (5, 8))):
         for c in mp_copies[stage * (nmp - 1):(stage + 1) * (nmp - 1)]:
             c.wait()
         for unit in range(lo, hi):
@@ -427,6 +482,9 @@
             value = prod[mp, unit].astype(F32)
             for k in range(nmp - 1):
                 value = value + prod_in[k, unit].astype(F32)
+            if t == 0:
+                here = (mp == 0) & (source == 0) & (iota(value.shape, 0) % 8 < steps)
+                value = jnp.where(here, row0, value)
             for c in range(2):
                 for k in range(heads):
                     at = (2 * c + t) * hs + k * steps
@@ -486,9 +544,11 @@
             pltpu.VMEM(pool.shape, BF16),
             pltpu.VMEM(w.shape, BF16),
             pltpu.VMEM((nseq,) + pp.shape, BF16),
-            pltpu.VMEM((hs, HEAD), BF16),
-            pltpu.VMEM((hs + 8, HEAD), F32),
-            pltpu.VMEM((hs + 8, HEAD), F32),
+            pltpu.VMEM((2, hs, HEAD), BF16),
+            pltpu.VMEM((2 * hs, HEAD), F32),
+            pltpu.VMEM((2, 2 * hs, HEAD), F32),
+            pltpu.VMEM((16, width // 2), BF16),
+            pltpu.VMEM((nmp - 1, 16, width // 2), BF16),
             pltpu.VMEM((hs, 128), F32),
             pltpu.VMEM((hs, 128), F32),
             pltpu.VMEM((128, 128), F32),
@@ -503,16 +563,17 @@
             pltpu.VMEM((nmp - 1, 8, 16, width // 2), BF16),
             pltpu.VMEM((4, 4 * hs, HEAD), F32),
             pltpu.VMEM(pq.shape, BF16),
-            dma((7,)),
+            dma((16,)),
             dma,
             dma((7,)), dma((7,)),
-            dma((3,)), dma((3,)),
+            dma((5,)), dma((5,)),
+            dma((nmp - 1,)), dma((nmp - 1,)),
             dma((2,)), dma((2,)),
             dma((2, 3)), dma((2, 3)),
             dma((3,)), dma((3,)),
             dma((2, 4)), dma((2, 4)),
             dma((2, 3)), dma((2, 3)),
-            dma((3, nmp - 1)), dma((3, nmp - 1)),
+            dma((4, nmp - 1)), dma((4, nmp - 1)),
         ],
         compiler_params=pltpu.CompilerParams(
             collective_id=0, has_side_effects=True, vmem_limit_bytes=56 * 1024 * 1024

time: 49.1 us -> 50.6 us (1.031)
  Pallas kernels: 48.4 us -> 49.8 us
    pallas_call x1, Pallas kernels: 46.5 us -> 47.9 us  [body(): pl.pallas_call(functools.partial(kernel, nsec, nseq, nmp, slots, rows, he...]
where the time goes in v4:
time: 50.6 us; the launch traced here: 50.4 us
  Pallas kernels  49.8 us (98%)
  between operations  0.64 us (1%)
    pallas_call x1, Pallas kernels, body(): pl.pallas_call(functools.partial(kernel, nsec, nseq, nmp, slots, rows, he...  47.9 us
    pallas_call x1, Pallas kernels, body(): pl.pallas_call(hand_over, out_shape=(jax.ShapeDtypeStruct(prefill.shape,...  1.91 us

profile of v4, /device:TPU:1, one launch (start us, length us, event | category | flops | bytes accessed | tf_op | source)
XLA Modules:
  0.0 50.4 jit_solution(13444832420769099111)
XLA Ops:
  0.6 47.9 %shard_map.95 = (bf16[2,128,1024]{2,1,0:T(8,128)(2,1)}, bf16[512,128]{1,0:T(8,128)(2,1)}) custom-call(bf16[2,128,1024]{2,1,0:T(8,128)(2,1)} %bitcast.19, bf16[512,128]{1,0:T(8,128)(2,1)} %bitcast.21, bf16[128,32,128]{2,1,0:T(8,128)(2,1)} %bitcast.18, bf16[1024,128]{1,0:T(8,128)(2,1)} %bitcast.20, bf16[12288,128]{1,0:T(8,128)(2,1)} %bitcast.16, ...), custom_call_target="tpu_custom_call" | custom-call | tf_op jit(solution)/shard_map/pallas_call | solution.py:531
  48.5 1.9 %shard_map.96 = (bf16[2,128,1024]{2,1,0:T(8,128)(2,1)}, bf16[512,128]{1,0:T(8,128)(2,1)}) custom-call(bf16[2,128,1024]{2,1,0:T(8,128)(2,1)} %get-tuple-element.6.pre_i, bf16[512,128]{1,0:T(8,128)(2,1)} %get-tuple-element.7.mix_i), custom_call_target="tpu_custom_call" | custom-call | tf_op jit(solution)/shard_map/pallas_call | solution.py:582

commit v5 on v4

--- a/solution.py
+++ b/solution.py
@@ -193,7 +193,7 @@
     q_second = remote(q0.at[0], q0.at[1], z_s.at[2], z_r.at[2], next_sec)
     q_first.start()
     kv_far = [remote(kv.at[me], kv.at[me], kv_s.at[i], kv_r.at[i], far[i]) for i in range(3)]
-    for c in kv_far:
+    for c in kv_far[:2]:
         c.start()
     kv_near = [remote(kv.at[me], kv.at[me], kv_s.at[3], kv_r.at[3], sibling)] + [
         remote(kv.at[2 * f + core], kv.at[2 * f + core], kv_s.at[4 + i], kv_r.at[4 + i], sibling)
@@ -258,15 +258,10 @@
             for c in st_copies:
                 c.start()
 
+    kv_far[2].start()
     q_first.wait()
     q_second.start()
 
-    for i in range(3):
-        kv_far[i].wait()
-        kv_near[i + 1].start()
-    for c in kv_near:
-        c.wait()
-    load_pq.wait()
     n = nseq * PAGE
 
     def prompt_keys(b):
@@ -274,20 +269,6 @@
 
     def prompt_values(b):
         return kv[:, (BLOCKS + b) * PAGE:(BLOCKS + b + 1) * PAGE, :].reshape(n, HEAD)
-
-    q_second.wait()
-    s0 = []
-    for b in range(BLOCKS):
-        scores = dot_nt(q0[1], prompt_keys(b))
-        s0.append(jnp.where(iota(scores.shape, 1) + b * n < ctx_s[0], scores, NEG))
-    m = functools.reduce(jnp.maximum, [jnp.max(x, axis=1, keepdims=True) for x in s0])
-    p0 = [jnp.exp2((x - m) * SCALE) for x in s0]
-    l = sum(jnp.sum(p, axis=1, keepdims=True) for p in p0)
-    r0_out[0:hs, :] = sum(dot_nn(p.astype(BF16), prompt_values(b)) for b, p in enumerate(p0))
-    r0_out[hs:2 * hs, :] = jnp.where(lane == 0, m, l)
-    r0_first = remote(r0_out, r0_in.at[0], z_s.at[3], z_r.at[3], next_sec)
-    r0_second = remote(r0_in.at[0], r0_in.at[1], z_s.at[4], z_r.at[4], next_sec)
-    r0_first.start()
 
     def prompt_piece(b, pair):
         two = pq_v[b, :, pl.ds(pl.multiple_of(pair * 2 * HEAD, 2 * HEAD), 2 * HEAD)]
@@ -319,7 +300,6 @@
         lax.fori_loop(lo, hi, step, 0)
 
     pairs = heads // 2
-    prompt_pieces(0, 0, 1)
 
     for c in st_copies:
         c.wait()
@@ -414,21 +394,50 @@
     ag_near[0].wait()
     products(0, [(order[0], chip)])
     send_products(0, 0, 1)
-    r0_first.wait()
-    r0_second.start()
     finish(order[1])
-    prompt_pieces(0, 1, 2)
+
+    for i in range(3):
+        kv_far[i].wait()
+        kv_near[i + 1].start()
+
     ag_near[1].wait()
     products(1, [(order[1], chip)])
     send_products(1, 1, 1)
-    prompt_pieces(0, 2, 3)
+    for c in kv_near:
+        c.wait()
+
+    q_second.wait()
+    s0 = []
+    for b in range(BLOCKS):
+        scores = dot_nt(q0[1], prompt_keys(b))
+        s0.append(jnp.where(iota(scores.shape, 1) + b * n < ctx_s[0], scores, NEG))
+    m = functools.reduce(jnp.maximum, [jnp.max(x, axis=1, keepdims=True) for x in s0])
+    p0 = [jnp.exp2((x - m) * SCALE) for x in s0]
+    l = sum(jnp.sum(p, axis=1, keepdims=True) for p in p0)
+    r0_out[0:hs, :] = sum(dot_nn(p.astype(BF16), prompt_values(b)) for b, p in enumerate(p0))
+    r0_out[hs:2 * hs, :] = jnp.where(lane == 0, m, l)
+    r0_first = remote(r0_out, r0_in.at[0], z_s.at[3], z_r.at[3], next_sec)
+    r0_second = remote(r0_in.at[0], r0_in.at[1], z_s.at[4], z_r.at[4], next_sec)
+    r0_first.start()
+
+    load_pq.wait()
+    prompt_pieces(0, 0, 1)
     forward = forward_rows(0)
-    prompt_pieces(0, 3, pairs)
+    prompt_pieces(0, 1, 2)
     for c in forward:
         c.wait()
     products(2, [(order[0], f) for f in from_chip])
     send_products(2, 2, 3)
+    r0_first.wait()
+    r0_second.start()
     forward = forward_rows(1)
+    prompt_pieces(0, 2, 3)
+    for c in forward:
+        c.wait()
+    products(5, [(order[1], f) for f in from_chip])
+    send_products(3, 5, 3)
+    prompt_pieces(0, 3, pairs)
+    prompt_pieces(1, 0, 1)
 
     r0_second.wait()
     prompt_m, prompt_l = r0_in[1, hs:2 * hs, 0:1], r0_in[1, hs:2 * hs, 1:2]
@@ -450,11 +459,7 @@
         def _(k=k):
             row0_copy(k).start()
 
-    for c in forward:
-        c.wait()
-    products(5, [(order[1], f) for f in from_chip])
-    send_products(3, 5, 3)
-    prompt_pieces(1, 0, pairs)
+    prompt_pieces(1, 1, pairs)
     pre_copy = pltpu.make_async_copy(pre_v, pre_h, out_sem)
     pre_copy.start()
 

time: 50.6 us -> 50.6 us (level)
  no operation moved by 1% of the time
where the time goes in v5:
time: 50.6 us; the launch traced here: 50.5 us
  Pallas kernels  49.8 us (98%)
  between operations  0.64 us (1%)
    pallas_call x1, Pallas kernels, body(): pl.pallas_call(functools.partial(kernel, nsec, nseq, nmp, slots, rows, he...  47.9 us
    pallas_call x1, Pallas kernels, body(): pl.pallas_call(hand_over, out_shape=(jax.ShapeDtypeStruct(prefill.shape,...  1.91 us

profile of v5, /device:TPU:1, one launch (start us, length us, event | category | flops | bytes accessed | tf_op | source)
XLA Modules:
  0.0 50.5 jit_solution(6210420300061379975)
XLA Ops:
  0.6 47.9 %shard_map.95 = (bf16[2,128,1024]{2,1,0:T(8,128)(2,1)}, bf16[512,128]{1,0:T(8,128)(2,1)}) custom-call(bf16[2,128,1024]{2,1,0:T(8,128)(2,1)} %bitcast.19, bf16[512,128]{1,0:T(8,128)(2,1)} %bitcast.21, bf16[128,32,128]{2,1,0:T(8,128)(2,1)} %bitcast.18, bf16[1024,128]{1,0:T(8,128)(2,1)} %bitcast.20, bf16[12288,128]{1,0:T(8,128)(2,1)} %bitcast.16, ...), custom_call_target="tpu_custom_call" | custom-call | tf_op jit(solution)/shard_map/pallas_call | solution.py:536
  48.5 1.9 %shard_map.96 = (bf16[2,128,1024]{2,1,0:T(8,128)(2,1)}, bf16[512,128]{1,0:T(8,128)(2,1)}) custom-call(bf16[2,128,1024]{2,1,0:T(8,128)(2,1)} %get-tuple-element.6.pre_i, bf16[512,128]{1,0:T(8,128)(2,1)} %get-tuple-element.7.mix_i), custom_call_target="tpu_custom_call" | custom-call | tf_op jit(solution)/shard_map/pallas_call | solution.py:587

commit v6 on v5

--- a/solution.py
+++ b/solution.py
@@ -50,8 +50,7 @@
     mp = lax.axis_index("mp")
     sec = lax.axis_index("section")
     chip, core = me // 2, me % 2
-    next_sec = {"section": lax.rem(sec + 1, nsec)}
-    last_sec = {"section": lax.rem(sec + nsec - 1, nsec)}
+    partner = {"section": lax.rem(sec + nsec // 2, nsec)}
     sibling = {"seq": 2 * chip + 1 - core}
     away = (1, 3, 2)
     far_chip = [lax.rem(chip + k, 4) for k in away]
@@ -68,7 +67,7 @@
         )
 
     barrier = pltpu.get_barrier_semaphore()
-    greeted = [*(mp_dev(k) for k in range(1, nmp)), next_sec, last_sec, *far, sibling]
+    greeted = [partner, *(mp_dev(k) for k in range(1, nmp)), *far, sibling]
     for device in greeted:
         pl.semaphore_signal(barrier, inc=1, device_id=device, device_id_type=MESH)
 
@@ -189,9 +188,8 @@
     pl.semaphore_wait(barrier, len(greeted))
     lse_copy = remote(lse_out, lse_in, z_s.at[0], z_r.at[0], sibling)
     lse_copy.start()
-    q_first = remote(dq_v.at[0], q0.at[0], z_s.at[1], z_r.at[1], next_sec)
-    q_second = remote(q0.at[0], q0.at[1], z_s.at[2], z_r.at[2], next_sec)
-    q_first.start()
+    q_copy = remote(dq_v.at[0], q0, z_s.at[1], z_r.at[1], partner)
+    q_copy.start()
     kv_far = [remote(kv.at[me], kv.at[me], kv_s.at[i], kv_r.at[i], far[i]) for i in range(3)]
     for c in kv_far[:2]:
         c.start()
@@ -259,8 +257,6 @@
                 c.start()
 
     kv_far[2].start()
-    q_first.wait()
-    q_second.start()
 
     n = nseq * PAGE
 
@@ -406,19 +402,18 @@
     for c in kv_near:
         c.wait()
 
-    q_second.wait()
+    q_copy.wait()
     s0 = []
     for b in range(BLOCKS):
-        scores = dot_nt(q0[1], prompt_keys(b))
+        scores = dot_nt(q0[...], prompt_keys(b))
         s0.append(jnp.where(iota(scores.shape, 1) + b * n < ctx_s[0], scores, NEG))
     m = functools.reduce(jnp.maximum, [jnp.max(x, axis=1, keepdims=True) for x in s0])
     p0 = [jnp.exp2((x - m) * SCALE) for x in s0]
     l = sum(jnp.sum(p, axis=1, keepdims=True) for p in p0)
     r0_out[0:hs, :] = sum(dot_nn(p.astype(BF16), prompt_values(b)) for b, p in enumerate(p0))
     r0_out[hs:2 * hs, :] = jnp.where(lane == 0, m, l)
-    r0_first = remote(r0_out, r0_in.at[0], z_s.at[3], z_r.at[3], next_sec)
-    r0_second = remote(r0_in.at[0], r0_in.at[1], z_s.at[4], z_r.at[4], next_sec)
-    r0_first.start()
+    r0_copy = remote(r0_out, r0_in, z_s.at[2], z_r.at[2], partner)
+    r0_copy.start()
 
     load_pq.wait()
     prompt_pieces(0, 0, 1)
@@ -428,8 +423,6 @@
         c.wait()
     products(2, [(order[0], f) for f in from_chip])
     send_products(2, 2, 3)
-    r0_first.wait()
-    r0_second.start()
     forward = forward_rows(1)
     prompt_pieces(0, 2, 3)
     for c in forward:
@@ -439,12 +432,12 @@
     prompt_pieces(0, 3, pairs)
     prompt_pieces(1, 0, 1)
 
-    r0_second.wait()
-    prompt_m, prompt_l = r0_in[1, hs:2 * hs, 0:1], r0_in[1, hs:2 * hs, 1:2]
+    r0_copy.wait()
+    prompt_m, prompt_l = r0_in[hs:2 * hs, 0:1], r0_in[hs:2 * hs, 1:2]
     peak = jnp.maximum(row0_m, prompt_m)
     keep = jnp.exp2((row0_m - peak) * SCALE)
     more = jnp.exp2((prompt_m - peak) * SCALE)
-    row0 = (row0_acc * keep + r0_in[1, 0:hs, :] * more) / (row0_l * keep + prompt_l * more)
+    row0 = (row0_acc * keep + r0_in[0:hs, :] * more) / (row0_l * keep + prompt_l * more)
     row0 = jnp.concatenate([row0[h * steps:(h + 1) * steps] for h in range(heads)], axis=1)
     row0 = jnp.concatenate([row0, jnp.zeros((16 - steps, row0.shape[1]), F32)], axis=0)
     row0 = dot_nn(row0.astype(BF16), w_v[...])[0:8]
@@ -549,9 +542,9 @@
             pltpu.VMEM(pool.shape, BF16),
             pltpu.VMEM(w.shape, BF16),
             pltpu.VMEM((nseq,) + pp.shape, BF16),
-            pltpu.VMEM((2, hs, HEAD), BF16),
+            pltpu.VMEM((hs, HEAD), BF16),
             pltpu.VMEM((2 * hs, HEAD), F32),
-            pltpu.VMEM((2, 2 * hs, HEAD), F32),
+            pltpu.VMEM((2 * hs, HEAD), F32),
             pltpu.VMEM((16, width // 2), BF16),
             pltpu.VMEM((nmp - 1, 16, width // 2), BF16),
             pltpu.VMEM((hs, 128), F32),
@@ -571,7 +564,7 @@
             dma((16,)),
             dma,
             dma((7,)), dma((7,)),
-            dma((5,)), dma((5,)),
+            dma((3,)), dma((3,)),
             dma((nmp - 1,)), dma((nmp - 1,)),
             dma((2,)), dma((2,)),
             dma((2, 3)), dma((2, 3)),

time: 50.6 us -> 48.3 us (0.955)
  Pallas kernels: 49.8 us -> 47.5 us
    pallas_call x1, Pallas kernels: 47.9 us -> 45.6 us  [body(): pl.pallas_call(functools.partial(kernel, nsec, nseq, nmp, slots, rows, he...]
where the time goes in v6:
time: 48.3 us; the launch traced here: 48.2 us
  Pallas kernels  47.5 us (98%)
  between operations  0.64 us (1%)
    pallas_call x1, Pallas kernels, body(): pl.pallas_call(functools.partial(kernel, nsec, nseq, nmp, slots, rows, he...  45.6 us
    pallas_call x1, Pallas kernels, body(): pl.pallas_call(hand_over, out_shape=(jax.ShapeDtypeStruct(prefill.shape,...  1.91 us

profile of v6, /device:TPU:1, one launch (start us, length us, event | category | flops | bytes accessed | tf_op | source)
XLA Modules:
  0.0 48.2 jit_solution(8703840366129239082)
XLA Ops:
  0.6 45.6 %shard_map.95 = (bf16[2,128,1024]{2,1,0:T(8,128)(2,1)}, bf16[512,128]{1,0:T(8,128)(2,1)}) custom-call(bf16[2,128,1024]{2,1,0:T(8,128)(2,1)} %bitcast.19, bf16[512,128]{1,0:T(8,128)(2,1)} %bitcast.21, bf16[128,32,128]{2,1,0:T(8,128)(2,1)} %bitcast.18, bf16[1024,128]{1,0:T(8,128)(2,1)} %bitcast.20, bf16[12288,128]{1,0:T(8,128)(2,1)} %bitcast.16, ...), custom_call_target="tpu_custom_call" | custom-call | tf_op jit(solution)/shard_map/pallas_call | solution.py:529
  46.3 1.9 %shard_map.96 = (bf16[2,128,1024]{2,1,0:T(8,128)(2,1)}, bf16[512,128]{1,0:T(8,128)(2,1)}) custom-call(bf16[2,128,1024]{2,1,0:T(8,128)(2,1)} %get-tuple-element.6.pre_i, bf16[512,128]{1,0:T(8,128)(2,1)} %get-tuple-element.7.mix_i), custom_call_target="tpu_custom_call" | custom-call | tf_op jit(solution)/shard_map/pallas_call | solution.py:580

commit v7 on v6

--- a/solution.py
+++ b/solution.py
@@ -191,7 +191,7 @@
     q_copy = remote(dq_v.at[0], q0, z_s.at[1], z_r.at[1], partner)
     q_copy.start()
     kv_far = [remote(kv.at[me], kv.at[me], kv_s.at[i], kv_r.at[i], far[i]) for i in range(3)]
-    for c in kv_far[:2]:
+    for c in kv_far:
         c.start()
     kv_near = [remote(kv.at[me], kv.at[me], kv_s.at[3], kv_r.at[3], sibling)] + [
         remote(kv.at[2 * f + core], kv.at[2 * f + core], kv_s.at[4 + i], kv_r.at[4 + i], sibling)
@@ -256,7 +256,6 @@
             for c in st_copies:
                 c.start()
 
-    kv_far[2].start()
 
     n = nseq * PAGE
 
@@ -386,19 +385,15 @@
         return copies
 
     finish(order[0])
+
+    for i in range(3):
+        kv_far[i].wait()
+        kv_near[i + 1].start()
+
     load_w.wait()
     ag_near[0].wait()
     products(0, [(order[0], chip)])
     send_products(0, 0, 1)
-    finish(order[1])
-
-    for i in range(3):
-        kv_far[i].wait()
-        kv_near[i + 1].start()
-
-    ag_near[1].wait()
-    products(1, [(order[1], chip)])
-    send_products(1, 1, 1)
     for c in kv_near:
         c.wait()
 
@@ -415,22 +410,23 @@
     r0_copy = remote(r0_out, r0_in, z_s.at[2], z_r.at[2], partner)
     r0_copy.start()
 
+    finish(order[1])
     load_pq.wait()
+    ag_near[1].wait()
+    products(1, [(order[1], chip)])
+    send_products(1, 1, 1)
+    forward = forward_rows(0)
     prompt_pieces(0, 0, 1)
-    forward = forward_rows(0)
-    prompt_pieces(0, 1, 2)
     for c in forward:
         c.wait()
     products(2, [(order[0], f) for f in from_chip])
     send_products(2, 2, 3)
     forward = forward_rows(1)
-    prompt_pieces(0, 2, 3)
     for c in forward:
         c.wait()
     products(5, [(order[1], f) for f in from_chip])
     send_products(3, 5, 3)
-    prompt_pieces(0, 3, pairs)
-    prompt_pieces(1, 0, 1)
+    prompt_pieces(0, 1, pairs)
 
     r0_copy.wait()
     prompt_m, prompt_l = r0_in[hs:2 * hs, 0:1], r0_in[hs:2 * hs, 1:2]
@@ -452,7 +448,7 @@
         def _(k=k):
             row0_copy(k).start()
 
-    prompt_pieces(1, 1, pairs)
+    prompt_pieces(1, 0, pairs)
     pre_copy = pltpu.make_async_copy(pre_v, pre_h, out_sem)
     pre_copy.start()
 

time: 48.3 us -> 47.3 us (0.979)
  Pallas kernels: 47.5 us -> 46.5 us
    pallas_call x1, Pallas kernels: 45.6 us -> 44.6 us  [body(): pl.pallas_call(functools.partial(kernel, nsec, nseq, nmp, slots, rows, he...]
where the time goes in v7:
time: 47.3 us; the launch traced here: 47.2 us
  Pallas kernels  46.5 us (98%)
  between operations  0.64 us (1%)
    pallas_call x1, Pallas kernels, body(): pl.pallas_call(functools.partial(kernel, nsec, nseq, nmp, slots, rows, he...  44.6 us
    pallas_call x1, Pallas kernels, body(): pl.pallas_call(hand_over, out_shape=(jax.ShapeDtypeStruct(prefill.shape,...  1.91 us

profile of v7, /device:TPU:1, one launch (start us, length us, event | category | flops | bytes accessed | tf_op | source)
XLA Modules:
  0.0 47.2 jit_solution(2326386281900066005)
XLA Ops:
  0.6 44.6 %shard_map.95 = (bf16[2,128,1024]{2,1,0:T(8,128)(2,1)}, bf16[512,128]{1,0:T(8,128)(2,1)}) custom-call(bf16[2,128,1024]{2,1,0:T(8,128)(2,1)} %bitcast.19, bf16[512,128]{1,0:T(8,128)(2,1)} %bitcast.21, bf16[128,32,128]{2,1,0:T(8,128)(2,1)} %bitcast.18, bf16[1024,128]{1,0:T(8,128)(2,1)} %bitcast.20, bf16[12288,128]{1,0:T(8,128)(2,1)} %bitcast.16, ...), custom_call_target="tpu_custom_call" | custom-call | tf_op jit(solution)/shard_map/pallas_call | solution.py:525
  45.3 1.9 %shard_map.96 = (bf16[2,128,1024]{2,1,0:T(8,128)(2,1)}, bf16[512,128]{1,0:T(8,128)(2,1)}) custom-call(bf16[2,128,1024]{2,1,0:T(8,128)(2,1)} %get-tuple-element.6.pre_i, bf16[512,128]{1,0:T(8,128)(2,1)} %get-tuple-element.7.mix_i), custom_call_target="tpu_custom_call" | custom-call | tf_op jit(solution)/shard_map/pallas_call | solution.py:576

commit v8 on v7

--- a/solution.py
+++ b/solution.py
@@ -175,16 +175,6 @@
         total > 0.0, top * SCALE + jnp.log2(jnp.maximum(total, 1e-30)), NEG
     )
     lse_out[...] = lse_mine
-    scores = dot_nt(dq_v[0], dp_v[0:2 * line, :])
-    ci = iota(scores.shape, 1)
-    allowed = (ci % 2 == 0) & (ci < line) & (ci // 2 <= iota(scores.shape, 0) % steps)
-    scores = jnp.where(allowed, scores, NEG)
-    row0_m = jnp.max(scores, axis=1, keepdims=True)
-    p = jnp.where(allowed, jnp.exp2((scores - row0_m) * SCALE), 0.0)
-    row0_l = jnp.sum(p, axis=1, keepdims=True)
-    p = jnp.concatenate([jnp.zeros((hs, 1), F32), p[:, :2 * line - 1]], axis=1)
-    row0_acc = dot_nn(p.astype(BF16), dp_v[0:2 * line, :])
-
     pl.semaphore_wait(barrier, len(greeted))
     lse_copy = remote(lse_out, lse_in, z_s.at[0], z_r.at[0], sibling)
     lse_copy.start()
@@ -201,6 +191,16 @@
     place_pick = jnp.where(
         iota((128, 128), 0) == jnp.broadcast_to(slot_place[0:1], (128, 128)), 1.0, 0.0
     )
+    scores = dot_nt(dq_v[0], dp_v[0:2 * line, :])
+    ci = iota(scores.shape, 1)
+    allowed = (ci % 2 == 0) & (ci < line) & (ci // 2 <= iota(scores.shape, 0) % steps)
+    scores = jnp.where(allowed, scores, NEG)
+    row0_m = jnp.max(scores, axis=1, keepdims=True)
+    p = jnp.where(allowed, jnp.exp2((scores - row0_m) * SCALE), 0.0)
+    row0_l = jnp.sum(p, axis=1, keepdims=True)
+    p = jnp.concatenate([jnp.zeros((hs, 1), F32), p[:, :2 * line - 1]], axis=1)
+    row0_acc = dot_nn(p.astype(BF16), dp_v[0:2 * line, :])
+
     lse_copy.wait()
     peak = jnp.maximum(lse_mine, lse_in[...])
     lse_chip = peak + jnp.log2(jnp.exp2(lse_mine - peak) + jnp.exp2(lse_in[...] - peak))
@@ -214,19 +214,25 @@
         weights = (place_pick * jnp.broadcast_to(factor[j:j + 1], (128, 128)))[:rows, :count]
         return dot_nn(weights.astype(BF16), accs[pl.ds(j, count, stride=hs), :].astype(BF16))
 
-    for i in range(half):
-        even, odd = row_sums(2 * i), row_sums(2 * i + 1)
-        for s in range(nseq):
-            for t in range(2):
-                sl = slice(s * own + 8 * t, s * own + 8 * t + 8)
-                part[t, s % 2, s // 2, i] = jnp.concatenate([even[sl], odd[sl]], axis=0).astype(BF16)
     order = (1, 0)
-    sib_copies = [
-        remote(part.at[t, 1 - core], sib_in.at[t], sib_s.at[t], sib_r.at[t], sibling)
-        for t in range(2)
-    ]
-    for t in order:
-        sib_copies[t].start()
+    sib_copies = [[], []]
+    for part_no in range(2):
+        lo, hi = part_no * half // 2, (part_no + 1) * half // 2
+        for i in range(lo, hi):
+            even, odd = row_sums(2 * i), row_sums(2 * i + 1)
+            for s in range(nseq):
+                for t in range(2):
+                    sl = slice(s * own + 8 * t, s * own + 8 * t + 8)
+                    part[t, s % 2, s // 2, i] = jnp.concatenate(
+                        [even[sl], odd[sl]], axis=0
+                    ).astype(BF16)
+        for t in order:
+            c = remote(
+                part.at[t, 1 - core, :, lo:hi], sib_in.at[t, :, lo:hi],
+                sib_s.at[t, part_no], sib_r.at[t, part_no], sibling,
+            )
+            c.start()
+            sib_copies[t].append(c)
 
     st_copies = [
         remote(
@@ -243,7 +249,8 @@
         for t in range(2)
     ]
     for t in order:
-        sib_copies[t].wait()
+        for c in sib_copies[t]:
+            c.wait()
         for i, f in enumerate(far_chip + [chip]):
             for at in range(0, half, 4):
                 sl = slice(at, at + 4)
@@ -562,7 +569,7 @@
             dma((7,)), dma((7,)),
             dma((3,)), dma((3,)),
             dma((nmp - 1,)), dma((nmp - 1,)),
-            dma((2,)), dma((2,)),
+            dma((2, 2)), dma((2, 2)),
             dma((2, 3)), dma((2, 3)),
             dma((3,)), dma((3,)),
             dma((2, 4)), dma((2, 4)),

time: 47.3 us -> 47.3 us (level)
  no operation moved by 1% of the time
where the time goes in v8:
time: 47.3 us; the launch traced here: 47.2 us
  Pallas kernels  46.6 us (99%)
  between operations  0.64 us (1%)
    pallas_call x1, Pallas kernels, body(): pl.pallas_call(functools.partial(kernel, nsec, nseq, nmp, slots, rows, he...  44.7 us
    pallas_call x1, Pallas kernels, body(): pl.pallas_call(hand_over, out_shape=(jax.ShapeDtypeStruct(prefill.shape,...  1.91 us

profile of v8, /device:TPU:1, one launch (start us, length us, event | category | flops | bytes accessed | tf_op | source)
XLA Modules:
  0.0 47.2 jit_solution(18417189537951343163)
XLA Ops:
  0.6 44.7 %shard_map.95 = (bf16[2,128,1024]{2,1,0:T(8,128)(2,1)}, bf16[512,128]{1,0:T(8,128)(2,1)}) custom-call(bf16[2,128,1024]{2,1,0:T(8,128)(2,1)} %bitcast.19, bf16[512,128]{1,0:T(8,128)(2,1)} %bitcast.21, bf16[128,32,128]{2,1,0:T(8,128)(2,1)} %bitcast.18, bf16[1024,128]{1,0:T(8,128)(2,1)} %bitcast.20, bf16[12288,128]{1,0:T(8,128)(2,1)} %bitcast.16, ...), custom_call_target="tpu_custom_call" | custom-call | tf_op jit(solution)/shard_map/pallas_call | solution.py:532
  45.3 1.9 %shard_map.96 = (bf16[2,128,1024]{2,1,0:T(8,128)(2,1)}, bf16[512,128]{1,0:T(8,128)(2,1)}) custom-call(bf16[2,128,1024]{2,1,0:T(8,128)(2,1)} %get-tuple-element.6.pre_i, bf16[512,128]{1,0:T(8,128)(2,1)} %get-tuple-element.7.mix_i), custom_call_target="tpu_custom_call" | custom-call | tf_op jit(solution)/shard_map/pallas_call | solution.py:583
